TPU v7x, 256 devices: a whole 4x4x8 slice. The times are simulated.
256 devices in a mesh: row: 8 (over z_lo, x), col: 32 (over z_hi, y, core).
Axes of the slice: x: 4, y: 4, z: 8 (z_hi: 4, z_lo: 2; z = z_hi * 2 + z_lo), core: 2. Of those that a mesh axis runs over, the one named last changes fastest.
Arguments:
- obj_start: float32 [2, 2048, 8192], P(None, 'row', 'col'), may hold values from -4 to 4
- probe_start: float32 [2, 128, 128], replicated, may hold values from -4 to 4
- amplitudes: bfloat16 [8, 32, 32, 128, 128], P('row', 'col'), may hold values from 0 to 2
- centres: int32 [2, 8, 32, 32], P(None, 'row', 'col'), may hold values from 0 to 255
- members: int32 [2, 8, 32, 32], P(None, 'row', 'col'), may hold values from 0 to 1, as said below
Outputs:
- obj_out: float32 [2, 2048, 8192], P(None, 'row', 'col')
- probe_out: float32 [2, 128, 128], replicated
Inputs may be any that keep to these rules, and one draw needn't show every extreme that they name: A slot belongs to at most one iteration's minibatch. In each iteration a device has at most 16 members, and some device has exactly 16 in every iteration.
All inputs are finite; a program needn't handle non-finite values.
Results may differ from a plain program's by a relative error of at most 0.0003.
Values sent between devices are 32-bit elements; how exact they have to be, the bound alone decides.
No kernel may reach another device: no remote copies, remote signals or barrier semaphores. Data moves between devices by JAX's collectives and lax.ppermute only.
A program may use at most 128 MiB of HBM per device.

v0:
```python
import math

import jax
import jax.numpy as jnp
from jax import lax
from jax.sharding import PartitionSpec as P

HIGH = lax.Precision.HIGHEST


def passed_along(array, axis, by):
    devices = lax.axis_size(axis)
    pairs = [(i, i + by) for i in range(devices) if 0 <= i + by < devices]
    return lax.ppermute(array, axis, pairs)


def extended_2(block, sides, width):
    for axis, dim in sides:
        count = lax.axis_size(axis)
        forward = [(i, i + 1) for i in range(count - 1)]
        backward = [(target, source) for source, target in forward]
        low = lax.ppermute(
            lax.slice_in_dim(block, block.shape[dim] - width, None, axis=dim), axis, forward
        )
        high = lax.ppermute(lax.slice_in_dim(block, 0, width, axis=dim), axis, backward)
        block = jnp.concatenate([low, block, high], axis=dim)
    return block


def tables(width):
    index = jnp.arange(width, dtype=jnp.int32)
    product = index[:, None] * index[None, :] % width
    angle = product.astype(jnp.float32) * (2.0 * math.pi / width)
    scale = 1.0 / math.sqrt(width)
    return (jnp.cos(angle) * scale, jnp.sin(angle) * scale)


def transform(field, cos_t, sin_t, sign):
    width = cos_t.shape[0]
    right = jnp.concatenate(
        [jnp.concatenate([cos_t, -sign * sin_t], 1), jnp.concatenate([sign * sin_t, cos_t], 1)], 0
    )
    field = jnp.einsum("brk,kl->brl", field, right, precision=HIGH)
    with_cos = jnp.einsum("jr,brk->bjk", cos_t, field, precision=HIGH)
    with_sin = jnp.einsum("jr,brk->bjk", sin_t, field, precision=HIGH)
    real_part = with_cos[..., :width] + sign * with_sin[..., width:]
    imag_part = with_cos[..., width:] - sign * with_sin[..., :width]
    return (real_part, imag_part)


def fold_rows(acc, tile, rim):
    from_below = passed_along(acc[:, :rim, :], "row", -1)
    from_above = passed_along(acc[:, rim + tile :, :], "row", 1)
    inner = acc[:, rim : rim + tile, :]
    inner = inner.at[:, tile - rim :, :].add(from_below)
    return inner.at[:, :rim, :].add(from_above)


def fold_cols(acc, tile, rim):
    from_right = passed_along(acc[:, :, :rim], "col", -1)
    from_left = passed_along(acc[:, :, rim + tile :], "col", 1)
    inner = acc[:, :, rim : rim + tile]
    inner = inner.at[:, :, tile - rim :].add(from_right)
    return inner.at[:, :, :rim].add(from_left)


def on_device(obj_start, probe_start, amplitudes, centres, members):
    tile = obj_start.shape[1]
    width = probe_start.shape[1]
    rim = width // 2
    iterations = members.shape[0]
    cos_t, sin_t = tables(width)
    amp_all = amplitudes[0, 0]
    rows_all = centres[0, 0, 0]
    cols_all = centres[1, 0, 0]
    obj = obj_start
    probe = probe_start
    for step in range(iterations):
        flags = members[step, 0, 0]
        wts = flags.astype(jnp.float32)
        extended = extended_2(obj, (("row", 1), ("col", 2)), rim)
        patches = jax.vmap(
            lambda top, left: lax.dynamic_slice(extended, (0, top, left), (2, width, width))
        )(rows_all, cols_all)
        obj_re = patches[:, 0]
        obj_im = patches[:, 1]
        pr = probe[0]
        pi = probe[1]
        wave = jnp.concatenate([pr * obj_re - pi * obj_im, pr * obj_im + pi * obj_re], -1)
        big_re, big_im = transform(wave, cos_t, sin_t, 1.0)
        mag = jnp.maximum(jnp.sqrt(big_re * big_re + big_im * big_im), 0.5)
        factor = (1.0 - amp_all.astype(jnp.float32) / mag) * wts[:, None, None]
        back_re, back_im = transform(
            jnp.concatenate([big_re * factor, big_im * factor], -1), cos_t, sin_t, -1.0
        )
        update = jnp.stack([pr * back_re + pi * back_im, pr * back_im - pi * back_re], 1)
        grad_p = jnp.stack(
            [
                jnp.sum(obj_re * back_re + obj_im * back_im, 0),
                jnp.sum(obj_re * back_im - obj_im * back_re, 0),
            ]
        )
        weight_p = jnp.sum(wts[:, None, None] * (obj_re * obj_re + obj_im * obj_im), 0)

        def place(slot, acc):
            start = (0, rows_all[slot], cols_all[slot])
            current = lax.dynamic_slice(acc, start, (2, width, width))
            return lax.dynamic_update_slice(acc, current + update[slot], start)

        acc = lax.fori_loop(0, update.shape[0], place, jnp.zeros_like(extended))
        grad_obj = fold_cols(fold_rows(acc, tile, rim), tile, rim)
        peak = jnp.max(pr * pr + pi * pi)
        obj = obj - grad_obj / (peak + 1e-06)
        grad_sum, weight_sum = lax.psum((grad_p, weight_p), ("row", "col"))
        probe = probe - grad_sum / (weight_sum + 1e-06)
    return (obj, probe)


def solution(mesh):
    in_specs = (
        P(None, "row", "col"),
        P(),
        P("row", "col", None, None, None),
        P(None, "row", "col", None),
        P(None, "row", "col", None),
    )
    out_specs = (P(None, "row", "col"), P())
    return jax.shard_map(
        on_device, mesh=mesh, in_specs=in_specs, out_specs=out_specs, check_vma=False
    )
```

profile of v0, /device:TPU:33, one launch (start us, length us, event | category | flops | bytes accessed | tf_op | source)
XLA Modules:
  0.0 1401.7 jit_solution(10665098652420192662)
XLA Ops:
  11.3 4.3 collective-permute-start.1
  19.8 4.3 collective-permute-start.2
  28.8 4.4 collective-permute-done.3
  36.2 82.8 %while.38 = (s32[]{:T(128)}, f32[2,384,384]{2,1,0:T(8,128)S(1)}, s32[32,3]{0,1:T(4,128)S(1)}, f32[32,2,128,128]{3,2,0,1:T(8,128)}, s32[]{:T(128)}) while((s32[]{:T(128)}, f32[2,384,384]{2,1,0:T(8,128)S(1)}, s32[32,3]{0,1:T(4,128)S(1)}, f32[32,2,128,128]{3,2,0,1:T(8,128)}, s32[]{:T(128)}) %tuple.145), condition=%wide.while_cond.8, body=%wide.while_body.8.sunk | while | flops 2 | bytes 263785 | solution.py:83
  121.9 4.3 fusion
  126.2 4.4 convolution_bitcast_fusion.6
  130.6 4.7 convolution_bitcast_fusion.7
  136.8 4.3 fusion.4
  145.3 4.6 convolution_bitcast_fusion.5
  155.2 273.7 %while.36 = (s32[]{:T(128)}, f32[2,384,384]{2,1,0:T(8,128)S(1)}, s32[32]{0:T(128)S(1)}, s32[32]{0:T(128)S(1)}, f32[32,2,128,128]{3,2,0,1:T(8,128)}, /*index=5*/s32[]{:T(128)}, s32[]{:T(128)}, s32[]{:T(128)}) while((s32[]{:T(128)}, f32[2,384,384]{2,1,0:T(8,128)S(1)}, s32[32]{0:T(128)S(1)}, s32[32]{0:T(128)S(1)}, f32[32,2,128,128]{3,2,0,1:T(8,128)}, ...), condition=%wide.region_1.2_spmd, body=%wide.region_0.1_spmd.sunk | while | flops 32776 | bytes 655553 | solution.py:110
  437.0 5.2 collective-permute-done.5
  446.0 243.1 %all-reduce.7.cloned.1.call-done = (f32[2,128,128]{2,1,0:T(8,128)}, f32[128,128]{1,0:T(8,128)}) async-done(((f32[2,128,128]{2,1,0:T(8,128)}, f32[128,128]{1,0:T(8,128)}), (f32[2,128,128]{2,1,0:T(8,128)}, f32[128,128]{1,0:T(8,128)})) %all-reduce.7.cloned.1.call-update) | async-done | bytes 196624 | tf_op jit(solution)/shard_map/psum | solution.py:114
  690.8 4.7 collective-permute-start.7
  704.1 4.6 collective-permute-start.9
  710.9 5.5 collective-permute-start.10
  721.1 4.4 collective-permute-done.11
  728.5 85.1 %while.39 = (s32[]{:T(128)}, f32[2,384,384]{2,1,0:T(8,128)S(1)}, s32[32,3]{0,1:T(4,128)S(1)}, f32[32,2,128,128]{3,2,0,1:T(8,128)}, s32[]{:T(128)}) while((s32[]{:T(128)}, f32[2,384,384]{2,1,0:T(8,128)S(1)}, s32[32,3]{0,1:T(4,128)S(1)}, f32[32,2,128,128]{3,2,0,1:T(8,128)}, s32[]{:T(128)}) %tuple.163), condition=%wide.while_cond.9, body=%wide.while_body.9.sunk | while | flops 2 | bytes 263785 | solution.py:83
  816.5 4.3 fusion.8
  820.8 4.4 convolution_bitcast_fusion.2
  825.3 4.7 convolution_bitcast_fusion.3
  835.7 4.4 convolution_bitcast_fusion
  840.1 4.7 convolution_bitcast_fusion.1
  850.1 273.7 %while.37 = (s32[]{:T(128)}, f32[2,384,384]{2,1,0:T(8,128)S(1)}, s32[32]{0:T(128)S(1)}, s32[32]{0:T(128)S(1)}, f32[32,2,128,128]{3,2,0,1:T(8,128)}, /*index=5*/s32[]{:T(128)}, s32[]{:T(128)}, s32[]{:T(128)}) while((s32[]{:T(128)}, f32[2,384,384]{2,1,0:T(8,128)S(1)}, s32[32]{0:T(128)S(1)}, s32[32]{0:T(128)S(1)}, ...), condition=%wide.region_9.10_spmd, body=%wide.region_8.9_spmd.sunk | while | flops 32776 | bytes 655553 | solution.py:110
  1130.6 250.0 %all-reduce.5.cloned.1.call-done = (f32[2,128,128]{2,1,0:T(8,128)}, f32[128,128]{1,0:T(8,128)}) async-done(((f32[2,128,128]{2,1,0:T(8,128)}, f32[128,128]{1,0:T(8,128)}), (f32[2,128,128]{2,1,0:T(8,128)}, f32[128,128]{1,0:T(8,128)})) %all-reduce.5.cloned.1.call-update) | async-done | bytes 196624 | tf_op jit(solution)/shard_map/psum | solution.py:114
  (573 shorter events, 558.8 us)
Async XLA Ops:
  7.2 18.9 %copy-start.15 = (s32[2,1,1,32]{3,2,1,0:T(1,128)S(1)}, s32[2,1,1,32]{3,2,1,0:T(1,128)}, u32[]{:S(2)}) copy-start(s32[2,1,1,32]{3,2,1,0:T(1,128)} %param.29) | copy-start | bytes 772
  7.2 682.0 %all-reduce.7.cloned.1.call-start = ((), (), s32[]{:S(2)}) async-start(), calls=%async_computation.1 | async-start | bytes 393216 | tf_op jit(solution)/shard_map/psum | solution.py:114
  8.2 10.3 collective-permute-start
  11.3 8.3 collective-permute-start.1
  15.9 120.9 %copy-start.4 = (f32[128,128]{1,0:T(8,128)}, f32[128,128]{1,0:T(8,128)S(1)}, u32[]{:S(2)}) copy-start(f32[128,128]{1,0:T(8,128)S(1)} %broadcast_multiply_fusion.1) | copy-start | bytes 196612
  18.5 118.3 %copy-start.6 = (f32[128,128]{1,0:T(8,128)}, f32[128,128]{1,0:T(8,128)S(1)}, u32[]{:S(2)}) copy-start(f32[128,128]{1,0:T(8,128)S(1)} %get-tuple-element.406) | copy-start | bytes 196612
  18.5 118.3 %copy-start.8 = (f32[128,128]{1,0:T(8,128)}, f32[128,128]{1,0:T(8,128)S(1)}, u32[]{:S(2)}) copy-start(f32[128,128]{1,0:T(8,128)S(1)} %get-tuple-element.407) | copy-start | bytes 196612
  19.8 9.0 collective-permute-start.2
  24.1 9.1 collective-permute-start.3
  155.2 277.0 %copy-start.10 = (f32[2,128,128]{2,1,0:T(8,128)S(1)}, f32[2,128,128]{2,1,0:T(8,128)}, u32[]{:S(2)}) copy-start(f32[2,128,128]{2,1,0:T(8,128)} %param.26) | copy-start | bytes 393220
  429.6 7.4 collective-permute-start.4
  433.5 8.6 collective-permute-start.5
  436.9 943.7 %all-reduce.5.cloned.1.call-start = ((), (), s32[]{:S(2)}) async-start(), calls=%async_computation | async-start | bytes 393216 | tf_op jit(solution)/shard_map/psum | solution.py:114
  444.0 257.2 %copy-start.3 = (f32[2,256,256]{2,1,0:T(8,128)S(1)}, f32[2,256,256]{2,1,0:T(8,128)}, u32[]{:S(2)}) copy-start(f32[2,256,256]{2,1,0:T(8,128)} %param.25) | copy-start | bytes 1572868
  444.0 251.5 %collective-permute-start.6 = (f32[2,256,64]{2,1,0:T(8,128)S(1)}, f32[2,256,64]{2,1,0:T(8,128)S(1)}, u32[]{:S(2)}, u32[]{:S(2)}) collective-permute-start(f32[2,256,64]{2,1,0:T(8,128)S(1)} %get-tuple-element.389), channel_id=1, source_target_pairs={{1,0},{2,1},{3,2},{4,3},{5,4},{6,5},{7,6},{8,7},{9,8},{10,9},{11,1... | collective-permute-start | bytes 393224 | tf_op jit(solution)/shard_map/ppermute | solution.py:14
  690.8 8.3 collective-permute-start.7
  701.3 8.7 collective-permute-start.8
  704.1 6.5 collective-permute-start.9
  710.9 10.2 collective-permute-start.10
  716.4 9.1 collective-permute-start.11
  1124.6 256.9 %collective-permute-start.12 = (f32[2,64,384]{2,1,0:T(8,128)S(1)}, f32[2,64,384]{2,1,0:T(8,128)S(1)}, u32[]{:S(2)}, u32[]{:S(2)}) collective-permute-start(f32[2,64,384]{2,1,0:T(8,128)S(1)} %get-tuple-element.381), channel_id=1, source_target_pairs={{32,0},{64,32},{96,64},{128,96},{160,128},{192,160},{224,192},{33,... | collective-permute-start | bytes 589832 | tf_op jit(solution)/shard_map/ppermute | solution.py:14
  1128.7 252.8 %collective-permute-start.13 = (f32[2,64,384]{2,1,0:T(8,128)S(1)}, f32[2,64,384]{2,1,0:T(8,128)S(1)}, u32[]{:S(2)}, u32[]{:S(2)}) collective-permute-start(f32[2,64,384]{2,1,0:T(8,128)S(1)} %get-tuple-element.380), channel_id=1, source_target_pairs={{0,32},{32,64},{64,96},{96,128},{128,160},{160,192},{192,224},{1,3... | collective-permute-start | bytes 589832 | tf_op jit(solution)/shard_map/ppermute | solution.py:14
  1381.7 8.7 collective-permute-start.14
  1385.9 6.6 collective-permute-start.15
  (10 other events, 66.7 us)
Sparse Core Ops, SparseCore 0:
  437.0 252.0 all-reduce.6
  1124.6 255.9 all-reduce.4
where the time goes:
time: 1420 us; the launch traced here: 1400 us
  waiting for transfers between devices  518 us (36%)
  local copies, waits for them, and re-layouts  415 us (29%)
  loops' own time  251 us (18%)
  other arithmetic  95.1 us (7%)
  matrix products  53.3 us (4%)
  starting transfers between devices  53.2 us (4%)
  between operations  16.4 us (1%)
    psum x2, waiting for transfers between devices, on_device(): grad_sum, weight_sum = lax.psum((grad_p, weight_p), ('row', 'col'))  493 us
    another operation x2, loops' own time, on_device(): acc = lax.fori_loop(0, update.shape[0], place, jnp.zeros_like(extended))  251 us
    gather x192, local copies, waits for them, and re-layouts  168 us
    dynamic_update_slice x64, local copies, waits for them, and re-layouts, place(): return lax.dynamic_update_slice(acc, current + update[slot], start)  156 us
    dynamic_slice x128, local copies, waits for them, and re-layouts, place(): start = (0, rows_all[slot], cols_all[slot])  75.2 us
    add x64, other arithmetic, place(): return lax.dynamic_update_slice(acc, current + update[slot], start)  65.3 us
  transfers between devices with their start and end apart: 18, of which 11 were waited for; matrix products, arithmetic and copies ran while one was open for 1% of the time, Pallas kernels for 0%

commit v1 on v0

v1 whole, which is shorter than its diff:
```python
import functools
import math

import jax
import jax.numpy as jnp
import numpy as np
from jax import lax
from jax.experimental import pallas as pl
from jax.experimental.pallas import tpu as pltpu
from jax.sharding import PartitionSpec as P

WIDTH = 128
RIM = WIDTH // 2
TILE = 256
EXT = TILE + WIDTH
BLOCKS = EXT // WIDTH
VMEM_LIMIT = 56 * 1024 * 1024


def dft_tables():
    index = np.arange(WIDTH)
    angle = (np.outer(index, index) % WIDTH) * (2.0 * math.pi / WIDTH)
    cos_t = np.cos(angle) / math.sqrt(WIDTH)
    sin_t = np.sin(angle) / math.sqrt(WIDTH)
    ahead = np.block([[cos_t, -sin_t], [sin_t, cos_t]])
    back = np.block([[cos_t, sin_t], [-sin_t, cos_t]])
    out = []
    for table in (ahead, back):
        high = table.astype(jnp.bfloat16)
        low = (table - high.astype(np.float64)).astype(jnp.bfloat16)
        out.append((high, low))
    (ah, al), (bh, bl) = out
    right_a = np.concatenate([ah, ah, al], 0)
    right_b = np.concatenate([bh, bh, bl], 0)
    left_a = np.concatenate([ah, ah, al], 1)
    left_b = np.concatenate([bh, bh, bl], 1)
    return right_a, left_b, left_a, right_b


def split(value):
    high = value.astype(jnp.bfloat16)
    low = (value - high.astype(jnp.float32)).astype(jnp.bfloat16)
    return high, low


def times_right(value, table):
    high, low = split(value)
    return jnp.dot(
        jnp.concatenate([high, low, high], 1), table, preferred_element_type=jnp.float32
    )


def times_left(table, value):
    high, low = split(value)
    return jnp.dot(
        table, jnp.concatenate([high, low, high], 0), preferred_element_type=jnp.float32
    )


def swap_halves(value):
    top, bottom = value[:WIDTH], value[WIDTH:]
    return jnp.concatenate(
        [
            jnp.concatenate([top[:, :WIDTH], bottom[:, :WIDTH]], 1),
            jnp.concatenate([top[:, WIDTH:], bottom[:, WIDTH:]], 1),
        ],
        0,
    )


def patterns_kernel(
    flags_ref, rows_ref, cols_ref, ext_ref, probe_ref, amp_ref,
    ra_ref, lb_ref, la_ref, rb_ref,
    acc_ref, sums_ref, slots_ref,
):
    cap = flags_ref.shape[0]
    slots_ref[0] = 0

    def note(slot, count):
        @pl.when(flags_ref[slot] != 0)
        def _():
            slots_ref[count] = slot

        return count + (flags_ref[slot] != 0).astype(jnp.int32)

    count = lax.fori_loop(0, cap, note, jnp.int32(0))
    acc_ref[...] = jnp.zeros_like(acc_ref)
    sums_ref[...] = jnp.zeros_like(sums_ref)
    lane = lax.broadcasted_iota(jnp.int32, (WIDTH, WIDTH), 1)

    def where_is(slot):
        left = cols_ref[slot]
        block = left // WIDTH
        return rows_ref[slot], block, left - block * WIDTH

    def patch(slot):
        top, block, shift = where_is(slot)
        parts = []
        for part in range(2):
            near = ext_ref[part, block, pl.ds(top, WIDTH), :]
            far = ext_ref[part, block + 1, pl.ds(top, WIDTH), :]
            merged = jnp.where(lane >= shift, near, far)
            parts.append(pltpu.roll(merged, (WIDTH - shift) % WIDTH, 1))
        return parts

    def place(slot, update):
        top, block, shift = where_is(slot)
        for part in range(2):
            rolled = pltpu.roll(update[part], shift, 1)
            acc_ref[part, block, pl.ds(top, WIDTH), :] += jnp.where(lane >= shift, rolled, 0.0)
            acc_ref[part, block + 1, pl.ds(top, WIDTH), :] += jnp.where(lane < shift, rolled, 0.0)

    def pair(index, carry):
        first = slots_ref[2 * index]
        real = 2 * index + 1 < count
        second = jnp.where(real, slots_ref[jnp.minimum(2 * index + 1, count - 1)], first)
        keep = real.astype(jnp.float32)
        pr, pi = probe_ref[0], probe_ref[1]
        waves = []
        objs = []
        for slot in (first, second):
            obj_re, obj_im = patch(slot)
            objs.append((obj_re, obj_im))
            waves.append(
                jnp.concatenate([pr * obj_re - pi * obj_im, pr * obj_im + pi * obj_re], 1)
            )
        field = times_right(jnp.concatenate(waves, 0), ra_ref[...])
        field = times_left(lb_ref[...], swap_halves(field))
        big_re, big_im = field[:WIDTH], field[WIDTH:]
        amp = jnp.concatenate(
            [amp_ref[first].astype(jnp.float32), amp_ref[second].astype(jnp.float32)], 1
        )
        inverse = jnp.minimum(lax.rsqrt(big_re * big_re + big_im * big_im), 2.0)
        factor = 1.0 - amp * inverse
        factor = jnp.concatenate([factor[:, :WIDTH], factor[:, WIDTH:] * keep], 1)
        chi = jnp.concatenate([big_re * factor, big_im * factor], 0)
        field = times_left(la_ref[...], chi)
        field = times_right(swap_halves(field), rb_ref[...])
        grads = [jnp.zeros((WIDTH, WIDTH), jnp.float32)] * 2
        weight = None
        for which, slot in enumerate((first, second)):
            part = field[which * WIDTH : (which + 1) * WIDTH]
            back_re, back_im = part[:, :WIDTH], part[:, WIDTH:]
            obj_re, obj_im = objs[which]
            place(slot, (pr * back_re + pi * back_im, pr * back_im - pi * back_re))
            grads[0] = grads[0] + (obj_re * back_re + obj_im * back_im)
            grads[1] = grads[1] + (obj_re * back_im - obj_im * back_re)
            power = obj_re * obj_re + obj_im * obj_im
            weight = power if weight is None else weight + keep * power
        sums_ref[0] += grads[0]
        sums_ref[1] += grads[1]
        sums_ref[2] += weight
        return carry

    lax.fori_loop(0, (count + 1) // 2, pair, jnp.int32(0))


def patterns(flags, rows, cols, ext, probe, amp, tables):
    smem = pl.BlockSpec(memory_space=pltpu.SMEM)
    vmem = pl.BlockSpec(memory_space=pltpu.VMEM)
    return pl.pallas_call(
        patterns_kernel,
        out_shape=(
            jax.ShapeDtypeStruct(ext.shape, jnp.float32),
            jax.ShapeDtypeStruct((3, WIDTH, WIDTH), jnp.float32),
        ),
        in_specs=[smem] * 3 + [vmem] * 7,
        out_specs=(vmem, vmem),
        scratch_shapes=[pltpu.SMEM((flags.shape[0],), jnp.int32)],
        compiler_params=pltpu.CompilerParams(vmem_limit_bytes=VMEM_LIMIT),
        name="patterns",
    )(flags, rows, cols, ext, probe, amp, *tables)


def edges(rows, cols):
    row = lax.axis_index("row")
    col = lax.axis_index("col")
    return jnp.stack([row > 0, row < rows - 1, col > 0, col < cols - 1]).astype(jnp.int32)


def assemble_kernel(edge_ref, obj_ref, up, down, left, right, ul, ur, dl, dr, ext_ref):
    lane = lax.broadcasted_iota(jnp.int32, (RIM, WIDTH), 1)
    low = lane < RIM
    has_up, has_down = edge_ref[0] != 0, edge_ref[1] != 0
    has_left, has_right = edge_ref[2] != 0, edge_ref[3] != 0

    def half(value):
        return pltpu.roll(value, RIM, 1)

    def gate(value, *conditions):
        for condition in conditions:
            value = jnp.where(condition, value, 0.0)
        return value

    def store(part, rows, mid, west, east):
        a, b = mid[:, :WIDTH], mid[:, WIDTH:]
        ra, rb = half(a), half(b)
        ext_ref[part, 0, rows, :] = jnp.where(low, west, ra)
        ext_ref[part, 1, rows, :] = jnp.where(low, ra, rb)
        ext_ref[part, 2, rows, :] = jnp.where(low, rb, half(east))

    for part in range(2):
        store(
            part, pl.ds(0, RIM), gate(up[part], has_up),
            gate(ul[part], has_up, has_left), gate(ur[part], has_up, has_right),
        )
        store(
            part, pl.ds(RIM + TILE, RIM), gate(down[part], has_down),
            gate(dl[part], has_down, has_left), gate(dr[part], has_down, has_right),
        )
        for step in range(TILE // RIM):
            rows = pl.ds((step % 2) * RIM, RIM)
            west = left[part, rows, :]
            east = right[part, rows, :]
            if step >= 2:
                west, east = half(west), half(east)
            store(
                part, pl.ds(RIM + step * RIM, RIM), obj_ref[part, pl.ds(step * RIM, RIM), :],
                gate(west, has_left), gate(east, has_right),
            )


def update_kernel(inner, edge_ref, probe_ref, ext_ref, acc_ref, up, down, left, right, ul, ur, dl, dr, out_ref):
    has_up, has_down = edge_ref[0] != 0, edge_ref[1] != 0
    has_left, has_right = edge_ref[2] != 0, edge_ref[3] != 0
    pr, pi = probe_ref[0], probe_ref[1]
    scale = 1.0 / (jnp.max(pr * pr + pi * pi) + 1e-06)
    lane = lax.broadcasted_iota(jnp.int32, (WIDTH, WIDTH), 1)
    row = lax.broadcasted_iota(jnp.int32, (WIDTH, WIDTH), 0)
    upper, west = row < RIM, lane < RIM

    def gate(value, *conditions):
        for condition in conditions:
            value = jnp.where(condition, value, 0.0)
        return value

    for part in range(2):
        new = {}
        for br in range(3):
            for bc in range(3):
                rows = pl.ds(br * WIDTH, WIDTH)
                total = acc_ref[part, bc, rows, :]
                vert = has_up if br == 0 else has_down
                hori = has_left if bc == 0 else has_right
                if br != 1:
                    total += gate((up if br == 0 else down)[part, bc], vert)
                if bc != 1:
                    total += gate((left if bc == 0 else right)[part, rows, :], hori)
                if br != 1 and bc != 1:
                    diagonal = {(0, 0): ul, (0, 2): ur, (2, 0): dl, (2, 2): dr}[(br, bc)]
                    total += gate(diagonal[part], vert, hori)
                value = ext_ref[part, bc, rows, :] - total * scale
                if not inner:
                    if br != 1:
                        value = jnp.where(jnp.logical_or(vert, (~upper) if br == 0 else upper), value, 0.0)
                    if bc != 1:
                        value = jnp.where(jnp.logical_or(hori, (~west) if bc == 0 else west), value, 0.0)
                    out_ref[part, bc, rows, :] = value
                new[br, bc] = value
        if inner:
            for br in range(3):
                turned = [pltpu.roll(new[br, bc], RIM, 1) for bc in range(3)]
                for half in range(2):
                    full = jnp.where(west, turned[half], turned[half + 1])
                    if br == 0:
                        out_ref[part, pl.ds(0, RIM), pl.ds(half * WIDTH, WIDTH)] = full[RIM:]
                    elif br == 1:
                        out_ref[part, pl.ds(RIM, WIDTH), pl.ds(half * WIDTH, WIDTH)] = full
                    else:
                        out_ref[part, pl.ds(RIM + WIDTH, RIM), pl.ds(half * WIDTH, WIDTH)] = full[:RIM]


def local_call(kernel, out, args, name):
    smem = pl.BlockSpec(memory_space=pltpu.SMEM)
    vmem = pl.BlockSpec(memory_space=pltpu.VMEM)
    return pl.pallas_call(
        kernel,
        out_shape=jax.ShapeDtypeStruct(out, jnp.float32),
        in_specs=[smem] + [vmem] * (len(args) - 1),
        out_specs=vmem,
        compiler_params=pltpu.CompilerParams(vmem_limit_bytes=VMEM_LIMIT),
        name=name,
    )(*args)


def on_device(rows_n, cols_n, obj, probe, amplitudes, centres, members):
    def shift(value, down, right):
        pairs = [
            (r * cols_n + c, (r + down) % rows_n * cols_n + (c + right) % cols_n)
            for r in range(rows_n)
            for c in range(cols_n)
        ]
        return lax.ppermute(value, ("row", "col"), pairs)

    def swap(value, row_bits, col_bits):
        pairs = [
            (r * cols_n + c, (r ^ row_bits) * cols_n + (c ^ col_bits))
            for r in range(rows_n)
            for c in range(cols_n)
        ]
        return lax.ppermute(value, ("row", "col"), pairs)

    tables = [jnp.asarray(table) for table in dft_tables()]
    amp = amplitudes[0, 0]
    rows = centres[0, 0, 0]
    cols = centres[1, 0, 0]
    edge = edges(rows_n, cols_n)
    core = lax.axis_index("col") % 2

    def lanes(strip):
        return jnp.concatenate([strip[:, :WIDTH], strip[:, WIDTH:]], 2)

    corner = lambda r, c: jnp.pad(obj[:, r : r + RIM, c : c + RIM], ((0, 0), (0, 0), (0, RIM)))
    far = TILE - RIM
    ext = local_call(
        assemble_kernel,
        (2, BLOCKS, EXT, WIDTH),
        (
            edge,
            obj,
            shift(obj[:, far:, :], 1, 0),
            shift(obj[:, :RIM, :], -1, 0),
            shift(lanes(obj[:, :, far:]), 0, 1),
            shift(lanes(obj[:, :, :RIM]), 0, -1),
            shift(corner(far, far), 1, 1),
            shift(corner(far, 0), 1, -1),
            shift(corner(0, far), -1, 1),
            shift(corner(0, 0), -1, -1),
        ),
        "assemble",
    )
    iterations = members.shape[0]
    for step in range(iterations):
        last = step == iterations - 1
        acc, sums = patterns(members[step, 0, 0], rows, cols, ext, probe, amp, tables)
        low, high = slice(0, WIDTH), slice(EXT - WIDTH, EXT)
        around = (
            shift(acc[:, :, high], 1, 0),
            shift(acc[:, :, low], -1, 0),
            shift(acc[:, 2], 0, 1),
            shift(acc[:, 0], 0, -1),
            shift(acc[:, 2, high], 1, 1),
            shift(acc[:, 0, high], 1, -1),
            shift(acc[:, 2, low], -1, 1),
            shift(acc[:, 0, low], -1, -1),
        )
        new_ext = local_call(
            functools.partial(update_kernel, last),
            obj.shape if last else ext.shape,
            (edge, probe, ext, acc) + around,
            "update",
        )
        mine = lax.dynamic_slice_in_dim(sums, core * RIM, RIM, 1)
        other = lax.dynamic_slice_in_dim(sums, (1 - core) * RIM, RIM, 1)
        total = mine + swap(other, 0, 1)
        for row_bits, col_bits in ((4, 0), (0, 8), (4, 24), (0, 2), (0, 6), (1, 0), (3, 0)):
            total = total + swap(total, row_bits, col_bits)
        held = lax.dynamic_slice_in_dim(probe, core * RIM, RIM, 1)
        held = held - total[:2] / (total[2] + 1e-06)
        other = swap(held, 0, 1)
        probe = jnp.where(
            core == 0,
            jnp.concatenate([held, other], 1),
            jnp.concatenate([other, held], 1),
        )
        ext = new_ext
    return ext, probe


def solution(mesh):
    in_specs = (
        P(None, "row", "col"),
        P(),
        P("row", "col", None, None, None),
        P(None, "row", "col", None),
        P(None, "row", "col", None),
    )
    out_specs = (P(None, "row", "col"), P())
    body = functools.partial(on_device, mesh.shape["row"], mesh.shape["col"])
    return jax.shard_map(
        body, mesh=mesh, in_specs=in_specs, out_specs=out_specs, check_vma=False
    )
```

time: 1420 us -> 226 us (0.16); the launches traced: 1400 us -> 226 us
  waiting for transfers between devices: 518 us -> 73.3 us
  local copies, waits for them, and re-layouts: 415 us -> 11.8 us
  loops' own time: 251 us -> 0 us
  other arithmetic: 95.1 us -> 4.23 us
  matrix products: 53.3 us -> 0 us
  starting transfers between devices: 53.2 us -> 103 us
  Pallas kernels: 0 us -> 32 us
  between operations: 16.4 us -> 1.26 us
    psum x2 -> x0, waiting for transfers between devices: 493 us -> none  [on_device(): grad_sum, weight_sum = lax.psum((grad_p, weight_p), ('row', 'col'))]
    another operation x4 -> x0, loops' own time: 251 us -> none  [the longest x2 251 us: on_device(): acc = lax.fori_loop(0, update.shape[0], place, jnp.zeros_like(extended))]
    gather x192 -> x0, local copies, waits for them, and re-layouts: 168 us -> none
    dynamic_update_slice x64 -> x0, local copies, waits for them, and re-layouts: 156 us -> none  [place(): return lax.dynamic_update_slice(acc, current + update[slot], start)]
    dynamic_slice x128 -> x2, local copies, waits for them, and re-layouts: 75.2 us -> 1.99 us  [on_device(): other = lax.dynamic_slice_in_dim(sums, (1 - core) * RIM, RIM, 1)]
    add x70 -> x16, other arithmetic: 68.8 us -> 1.99 us  [the longest x2 1.81 us: on_device(): total = mine + swap(other, 0, 1)]
    dot_general x12 -> x0, matrix products: 53.3 us -> none  [the longest x4 18.7 us: transform(): with_cos = jnp.einsum('jr,brk->bjk', cos_t, field, precision=HIGH)]
    ppermute x16 -> x42, starting transfers between devices: 53.1 us -> 103 us  [the longest x24 58.4 us: shift(): return lax.ppermute(value, ('row', 'col'), pairs)]
  transfers between devices with their start and end apart: 18 -> 42, of which waited for: 11 -> 17; matrix products, arithmetic and copies ran while one was open for 1% -> 1% of each run, Pallas kernels for 0% -> 3%
where the time goes in v1:
time: 226 us
  starting transfers between devices  103 us (46%)
  waiting for transfers between devices  73.3 us (32%)
  Pallas kernels  32 us (14%)
  local copies, waits for them, and re-layouts  11.8 us (5%)
  other arithmetic  4.23 us (2%)
    ppermute x24, starting transfers between devices, shift(): return lax.ppermute(value, ('row', 'col'), pairs)  58.4 us
    ppermute x18, starting transfers between devices, swap(): return lax.ppermute(value, ('row', 'col'), pairs)  44.8 us
    ppermute x18, waiting for transfers between devices, swap(): return lax.ppermute(value, ('row', 'col'), pairs)  42.4 us
    ppermute x24, waiting for transfers between devices, shift(): return lax.ppermute(value, ('row', 'col'), pairs)  31 us
    pallas_call x2, Pallas kernels, patterns(): pl.pallas_call(patterns_kernel, out_shape=(jax.ShapeDtypeStruct(ext.shape...  22 us
    pallas_call x3, Pallas kernels, local_call(): pl.pallas_call(kernel, out_shape=jax.ShapeDtypeStruct(out, jnp.float32),...  10 us
    unnamed x62, local copies, waits for them, and re-layouts  6.71 us
  transfers between devices with their start and end apart: 42, of which 17 were waited for; matrix products, arithmetic and copies ran while one was open for 1% of the time, Pallas kernels for 3%

profile of v1, /device:TPU:33, one launch (start us, length us, event | category | flops | bytes accessed | tf_op | source)
XLA Modules:
  0.0 225.9 jit_solution(7165259005478711076)
XLA Ops:
  4.8 4.8 %collective-permute-start.6 = (f32[2,64,128]{2,1,0:T(8,128)S(1)}, f32[2,64,128]{2,1,0:T(8,128)S(1)}, u32[]{:S(2)}, u32[]{:S(2)}) collective-permute-start(f32[2,64,128]{2,1,0:T(8,128)S(1)} %pad.15), channel_id=1, source_target_pairs={{0,225},{1,226},{2,227},{3,228},{4,229},{5,230},{6,231},{7,232},{8... | collective-permute-start | bytes 196616 | tf_op jit(solution)/shard_map/ppermute | solution.py:293
  15.3 10.4 %collective-permute-start.7 = (f32[2,64,128]{2,1,0:T(8,128)S(1)}, f32[2,64,128]{2,1,0:T(8,128)S(1)}, u32[]{:S(2)}, u32[]{:S(2)}) collective-permute-start(f32[2,64,128]{2,1,0:T(8,128)S(1)} %pad.16), channel_id=1, source_target_pairs={{0,255},{1,224},{2,225},{3,226},{4,227},{5,228},{6,229},{7,230},{8... | collective-permute-start | bytes 196616 | tf_op jit(solution)/shard_map/ppermute | solution.py:293
  29.2 2.9 %assemble.1.ext_ref = f32[2,3,384,128]{3,2,1,0:T(8,128)} custom-call(s32[4]{0:T(128)} %add_convert_fusion.edge_ref, f32[2,256,256]{2,1,0:T(8,128)} %obj_ref.1, f32[2,64,256]{2,1,0:T(8,128)} %copy-done.18, f32[2,64,256]{2,1,0:T(8,128)} %copy-done.17, f32[2,128,128]{2,1,0:T(8,128)} %copy-done.19, f32[2,128,128]{2,1,0:T(8,128)} %copy-done.20, ...), custom_call_target="tpu_custom_call" | custom-call | tf_op jit(solution)/shard_map/assemble/pallas_call | solution.py:276
  32.1 11.0 %patterns.2 = (f32[2,3,384,128]{3,2,1,0:T(8,128)}, f32[3,128,128]{2,1,0:T(8,128)}) custom-call(s32[32]{0:T(128)} %get-tuple-element.37.flags_ref, s32[32]{0:T(128)} %get-tuple-element.40.rows_ref, s32[32]{0:T(128)} %get-tuple-element.41.cols_ref, f32[2,3,384,128]{3,2,1,0:T(8,128)} %assemble.1.ext_ref, f32[2,128,128]{2,1,0:T(8,128)} %probe_ref.3, ...), custom_call_target="tpu_custom_call" | custom-call | tf_op jit(solution)/shard_map/patterns/pallas_call | solution.py:161
  50.8 4.4 %collective-permute-done.10 = f32[3,64,128]{2,1,0:T(8,128)S(1)} collective-permute-done((f32[3,64,128]{2,1,0:T(8,128)S(1)}, f32[3,64,128]{2,1,0:T(8,128)S(1)}, u32[]{:S(2)}, u32[]{:S(2)}) %collective-permute-start.10) | collective-permute-done | bytes 98336 | tf_op jit(solution)/shard_map/ppermute | solution.py:301
  55.3 8.5 %collective-permute-start.11 = (f32[3,64,128]{2,1,0:T(8,128)S(1)}, f32[3,64,128]{2,1,0:T(8,128)S(1)}, u32[]{:S(2)}, u32[]{:S(2)}) collective-permute-start(f32[3,64,128]{2,1,0:T(8,128)S(1)} %add.83), channel_id=1, source_target_pairs={{0,152},{1,153},{2,154},{3,155},{4,156},{5,157},{6,158},{7,159},{8... | collective-permute-start | bytes 294920 | tf_op jit(solution)/shard_map/ppermute | solution.py:301
  66.6 3.5 %collective-permute-done.12 = f32[3,64,128]{2,1,0:T(8,128)S(1)} collective-permute-done((f32[3,64,128]{2,1,0:T(8,128)S(1)}, f32[3,64,128]{2,1,0:T(8,128)S(1)}, u32[]{:S(2)}, u32[]{:S(2)}) %collective-permute-start.12) | collective-permute-done | bytes 98336 | tf_op jit(solution)/shard_map/ppermute | solution.py:301
  75.9 11.1 %collective-permute-start.24 = (f32[2,128,128]{2,1,0:T(8,128)S(1)}, f32[2,128,128]{2,1,0:T(8,128)S(1)}, u32[]{:S(2)}, u32[]{:S(2)}) collective-permute-start(f32[2,128,128]{2,1,0:T(8,128)S(1)} %get-tuple-element.18), channel_id=1, source_target_pairs={{0,255},{1,224},{2,225},{3,226},{4,227},{5,228},{6,229},{7,230},{8... | collective-permute-start | bytes 393224 | tf_op jit(solution)/shard_map/ppermute | solution.py:293
  87.2 4.9 %collective-permute-start.22 = (f32[2,128,128]{2,1,0:T(8,128)S(1)}, f32[2,128,128]{2,1,0:T(8,128)S(1)}, u32[]{:S(2)}, u32[]{:S(2)}) collective-permute-start(f32[2,128,128]{2,1,0:T(8,128)S(1)} %get-tuple-element.20), channel_id=1, source_target_pairs={{0,63},{1,32},{2,33},{3,34},{4,35},{5,36},{6,37},{7,38},{8,39},{9,... | collective-permute-start | bytes 393224 | tf_op jit(solution)/shard_map/ppermute | solution.py:293
  99.0 15.1 %collective-permute-done.21.ul = f32[2,128,128]{2,1,0:T(8,128)S(1)} collective-permute-done((f32[2,128,128]{2,1,0:T(8,128)S(1)}, f32[2,128,128]{2,1,0:T(8,128)S(1)}, u32[]{:S(2)}, u32[]{:S(2)}) %collective-permute-start.21) | collective-permute-done | bytes 131104 | tf_op jit(solution)/shard_map/ppermute | solution.py:293
  114.8 12.5 %collective-permute-start.16 = (f32[2,64,128]{2,1,0:T(8,128)S(1)}, f32[2,64,128]{2,1,0:T(8,128)S(1)}, u32[]{:S(2)}, u32[]{:S(2)}) collective-permute-start(f32[2,64,128]{2,1,0:T(8,128)S(1)} %fusion.1), channel_id=1, source_target_pairs={{0,1},{1,0},{2,3},{3,2},{4,5},{5,4},{6,7},{7,6},{8,9},{9,8},{10,11... | collective-permute-start | bytes 196616 | tf_op jit(solution)/shard_map/ppermute | solution.py:301
  129.1 3.6 %update.2.ext_ref = f32[2,3,384,128]{3,2,1,0:T(8,128)} custom-call(s32[4]{0:T(128)} %add_convert_fusion.edge_ref, f32[2,128,128]{2,1,0:T(8,128)} %probe_ref.3, f32[2,3,384,128]{3,2,1,0:T(8,128)} %assemble.1.ext_ref, f32[2,3,384,128]{3,2,1,0:T(8,128)} %get-tuple-element.7.acc_ref, f32[2,3,128,128]{3,2,1,0:T(8,128)} %copy-done.8, ...), custom_call_target="tpu_custom_call" | custom-call | tf_op jit(solution)/shard_map/update/pallas_call | solution.py:276
  133.4 11.0 %patterns.3 = (f32[2,3,384,128]{3,2,1,0:T(8,128)}, f32[3,128,128]{2,1,0:T(8,128)}) custom-call(s32[32]{0:T(128)} %get-tuple-element.36.flags_ref, s32[32]{0:T(128)} %get-tuple-element.40.rows_ref, s32[32]{0:T(128)} %get-tuple-element.41.cols_ref, f32[2,3,384,128]{3,2,1,0:T(8,128)} %update.2.ext_ref, f32[2,128,128]{2,1,0:T(8,128)} %maximum_select_fusion.probe_ref, ...), custom_call_target="tpu_custom_call" | custom-call | tf_op jit(solution)/shard_map/patterns/pallas_call | solution.py:161
  147.7 4.2 %collective-permute-done.34 = f32[3,64,128]{2,1,0:T(8,128)S(1)} collective-permute-done((f32[3,64,128]{2,1,0:T(8,128)S(1)}, f32[3,64,128]{2,1,0:T(8,128)S(1)}, u32[]{:S(2)}, u32[]{:S(2)}) %collective-permute-start.34) | collective-permute-done | bytes 98336 | tf_op jit(solution)/shard_map/ppermute | solution.py:301
  152.1 4.6 %collective-permute-done.35 = f32[3,64,128]{2,1,0:T(8,128)S(1)} collective-permute-done((f32[3,64,128]{2,1,0:T(8,128)S(1)}, f32[3,64,128]{2,1,0:T(8,128)S(1)}, u32[]{:S(2)}, u32[]{:S(2)}) %collective-permute-start.35) | collective-permute-done | bytes 98336 | tf_op jit(solution)/shard_map/ppermute | solution.py:301
  159.5 3.7 %collective-permute-done.36 = f32[3,64,128]{2,1,0:T(8,128)S(1)} collective-permute-done((f32[3,64,128]{2,1,0:T(8,128)S(1)}, f32[3,64,128]{2,1,0:T(8,128)S(1)}, u32[]{:S(2)}, u32[]{:S(2)}) %collective-permute-start.36) | collective-permute-done | bytes 98336 | tf_op jit(solution)/shard_map/ppermute | solution.py:301
  163.3 3.5 %collective-permute-done.37 = f32[3,64,128]{2,1,0:T(8,128)S(1)} collective-permute-done((f32[3,64,128]{2,1,0:T(8,128)S(1)}, f32[3,64,128]{2,1,0:T(8,128)S(1)}, u32[]{:S(2)}, u32[]{:S(2)}) %collective-permute-start.37) | collective-permute-done | bytes 98336 | tf_op jit(solution)/shard_map/ppermute | solution.py:301
  167.0 4.6 %collective-permute-done.38 = f32[3,64,128]{2,1,0:T(8,128)S(1)} collective-permute-done((f32[3,64,128]{2,1,0:T(8,128)S(1)}, f32[3,64,128]{2,1,0:T(8,128)S(1)}, u32[]{:S(2)}, u32[]{:S(2)}) %collective-permute-start.38) | collective-permute-done | bytes 98336 | tf_op jit(solution)/shard_map/ppermute | solution.py:301
  176.9 5.7 %collective-permute-start.30 = (f32[2,128,128]{2,1,0:T(8,128)S(1)}, f32[2,128,128]{2,1,0:T(8,128)S(1)}, u32[]{:S(2)}, u32[]{:S(2)}) collective-permute-start(f32[2,128,128]{2,1,0:T(8,128)S(1)} %get-tuple-element.12), channel_id=1, source_target_pairs={{0,63},{1,32},{2,33},{3,34},{4,35},{5,36},{6,37},{7,38},{8,39},{9,... | collective-permute-start | bytes 393224 | tf_op jit(solution)/shard_map/ppermute | solution.py:293
  182.6 3.8 %collective-permute-start.28 = (f32[2,384,128]{2,1,0:T(8,128)S(1)}, f32[2,384,128]{2,1,0:T(8,128)S(1)}, u32[]{:S(2)}, u32[]{:S(2)}) collective-permute-start(f32[2,384,128]{2,1,0:T(8,128)S(1)} %get-tuple-element.14), channel_id=1, source_target_pairs={{0,31},{1,0},{2,1},{3,2},{4,3},{5,4},{6,5},{7,6},{8,7},{9,8},{10,9... | collective-permute-start | bytes 1179656 | tf_op jit(solution)/shard_map/ppermute | solution.py:293
  186.4 3.7 %collective-permute-start.27 = (f32[2,384,128]{2,1,0:T(8,128)S(1)}, f32[2,384,128]{2,1,0:T(8,128)S(1)}, u32[]{:S(2)}, u32[]{:S(2)}) collective-permute-start(f32[2,384,128]{2,1,0:T(8,128)S(1)} %get-tuple-element.15), channel_id=1, source_target_pairs={{0,1},{1,2},{2,3},{3,4},{4,5},{5,6},{6,7},{7,8},{8,9},{9,10},{10,1... | collective-permute-start | bytes 1179656 | tf_op jit(solution)/shard_map/ppermute | solution.py:293
  191.8 14.3 %collective-permute-done.29.ul = f32[2,128,128]{2,1,0:T(8,128)S(1)} collective-permute-done((f32[2,128,128]{2,1,0:T(8,128)S(1)}, f32[2,128,128]{2,1,0:T(8,128)S(1)}, u32[]{:S(2)}, u32[]{:S(2)}) %collective-permute-start.29) | collective-permute-done | bytes 131104 | tf_op jit(solution)/shard_map/ppermute | solution.py:293
  206.1 13.9 %collective-permute-start.41 = (f32[2,64,128]{2,1,0:T(8,128)S(1)}, f32[2,64,128]{2,1,0:T(8,128)S(1)}, u32[]{:S(2)}, u32[]{:S(2)}) collective-permute-start(f32[2,64,128]{2,1,0:T(8,128)S(1)} %fusion), channel_id=1, source_target_pairs={{0,1},{1,0},{2,3},{3,2},{4,5},{5,4},{6,7},{7,6},{8,9},{9,8},{10,11... | collective-permute-start | bytes 196616 | tf_op jit(solution)/shard_map/ppermute | solution.py:301
  221.8 3.5 %update.3 = f32[2,256,256]{2,1,0:T(8,128)} custom-call(s32[4]{0:T(128)} %add_convert_fusion.edge_ref, f32[2,128,128]{2,1,0:T(8,128)} %maximum_select_fusion.probe_ref, f32[2,3,384,128]{3,2,1,0:T(8,128)} %update.2.ext_ref, f32[2,3,384,128]{3,2,1,0:T(8,128)} %get-tuple-element.8.acc_ref, f32[2,3,128,128]{3,2,1,0:T(8,128)} %copy-done.12, ...), custom_call_target="tpu_custom_call" | custom-call | tf_op jit(solution)/shard_map/update/pallas_call | solution.py:276
  (168 shorter events, 55.6 us)
Async XLA Ops:
  10.6 17.3 %collective-permute-start.1 = (f32[2,64,256]{2,1,0:T(8,128)S(1)}, f32[2,64,256]{2,1,0:T(8,128)S(1)}, u32[]{:S(2)}, u32[]{:S(2)}) collective-permute-start(f32[2,64,256]{2,1,0:T(8,128)S(1)} %get-tuple-element.34), channel_id=1, source_target_pairs={{0,224},{1,225},{2,226},{3,227},{4,228},{5,229},{6,230},{7,231},{8... | collective-permute-start | bytes 393224 | tf_op jit(solution)/shard_map/ppermute | solution.py:293
  10.9 16.9 %collective-permute-start = (f32[2,64,256]{2,1,0:T(8,128)S(1)}, f32[2,64,256]{2,1,0:T(8,128)S(1)}, u32[]{:S(2)}, u32[]{:S(2)}) collective-permute-start(f32[2,64,256]{2,1,0:T(8,128)S(1)} %get-tuple-element.35), channel_id=1, source_target_pairs={{0,32},{1,33},{2,34},{3,35},{4,36},{5,37},{6,38},{7,39},{8,40},{9,... | collective-permute-start | bytes 393224 | tf_op jit(solution)/shard_map/ppermute | solution.py:293
  12.5 15.4 %collective-permute-start.2 = (f32[2,128,128]{2,1,0:T(8,128)S(1)}, f32[2,128,128]{2,1,0:T(8,128)S(1)}, u32[]{:S(2)}, u32[]{:S(2)}) collective-permute-start(f32[2,128,128]{2,1,0:T(8,128)S(1)} %pad_maximum_fusion), channel_id=1, source_target_pairs={{0,1},{1,2},{2,3},{3,4},{4,5},{5,6},{6,7},{7,8},{8,9},{9,10},{10,1... | collective-permute-start | bytes 393224 | tf_op jit(solution)/shard_map/ppermute | solution.py:293
  12.6 15.3 %collective-permute-start.3 = (f32[2,128,128]{2,1,0:T(8,128)S(1)}, f32[2,128,128]{2,1,0:T(8,128)S(1)}, u32[]{:S(2)}, u32[]{:S(2)}) collective-permute-start(f32[2,128,128]{2,1,0:T(8,128)S(1)} %pad_maximum_fusion.1), channel_id=1, source_target_pairs={{0,31},{1,0},{2,1},{3,2},{4,3},{5,4},{6,5},{7,6},{8,7},{9,8},{10,9... | collective-permute-start | bytes 393224 | tf_op jit(solution)/shard_map/ppermute | solution.py:293
  15.3 12.6 %collective-permute-start.7 = (f32[2,64,128]{2,1,0:T(8,128)S(1)}, f32[2,64,128]{2,1,0:T(8,128)S(1)}, u32[]{:S(2)}, u32[]{:S(2)}) collective-permute-start(f32[2,64,128]{2,1,0:T(8,128)S(1)} %pad.16), channel_id=1, source_target_pairs={{0,255},{1,224},{2,225},{3,226},{4,227},{5,228},{6,229},{7,230},{8... | collective-permute-start | bytes 196616 | tf_op jit(solution)/shard_map/ppermute | solution.py:293
  55.3 11.2 %collective-permute-start.11 = (f32[3,64,128]{2,1,0:T(8,128)S(1)}, f32[3,64,128]{2,1,0:T(8,128)S(1)}, u32[]{:S(2)}, u32[]{:S(2)}) collective-permute-start(f32[3,64,128]{2,1,0:T(8,128)S(1)} %add.83), channel_id=1, source_target_pairs={{0,152},{1,153},{2,154},{3,155},{4,156},{5,157},{6,158},{7,159},{8... | collective-permute-start | bytes 294920 | tf_op jit(solution)/shard_map/ppermute | solution.py:301
  74.8 12.2 %collective-permute-start.14 = (f32[3,64,128]{2,1,0:T(8,128)S(1)}, f32[3,64,128]{2,1,0:T(8,128)S(1)}, u32[]{:S(2)}, u32[]{:S(2)}) collective-permute-start(f32[3,64,128]{2,1,0:T(8,128)S(1)} %add.86), channel_id=1, source_target_pairs={{0,32},{1,33},{2,34},{3,35},{4,36},{5,37},{6,38},{7,39},{8,40},{9,... | collective-permute-start | bytes 294920 | tf_op jit(solution)/shard_map/ppermute | solution.py:301
  75.9 19.2 %collective-permute-start.24 = (f32[2,128,128]{2,1,0:T(8,128)S(1)}, f32[2,128,128]{2,1,0:T(8,128)S(1)}, u32[]{:S(2)}, u32[]{:S(2)}) collective-permute-start(f32[2,128,128]{2,1,0:T(8,128)S(1)} %get-tuple-element.18), channel_id=1, source_target_pairs={{0,255},{1,224},{2,225},{3,226},{4,227},{5,228},{6,229},{7,230},{8... | collective-permute-start | bytes 393224 | tf_op jit(solution)/shard_map/ppermute | solution.py:293
  87.2 11.1 %collective-permute-start.22 = (f32[2,128,128]{2,1,0:T(8,128)S(1)}, f32[2,128,128]{2,1,0:T(8,128)S(1)}, u32[]{:S(2)}, u32[]{:S(2)}) collective-permute-start(f32[2,128,128]{2,1,0:T(8,128)S(1)} %get-tuple-element.20), channel_id=1, source_target_pairs={{0,63},{1,32},{2,33},{3,34},{4,35},{5,36},{6,37},{7,38},{8,39},{9,... | collective-permute-start | bytes 393224 | tf_op jit(solution)/shard_map/ppermute | solution.py:293
  92.1 35.1 %collective-permute-start.20 = (f32[2,384,128]{2,1,0:T(8,128)S(1)}, f32[2,384,128]{2,1,0:T(8,128)S(1)}, u32[]{:S(2)}, u32[]{:S(2)}) collective-permute-start(f32[2,384,128]{2,1,0:T(8,128)S(1)} %get-tuple-element.22), channel_id=1, source_target_pairs={{0,31},{1,0},{2,1},{3,2},{4,3},{5,4},{6,5},{7,6},{8,7},{9,8},{10,9... | collective-permute-start | bytes 1179656 | tf_op jit(solution)/shard_map/ppermute | solution.py:293
  95.1 32.2 %collective-permute-start.19 = (f32[2,384,128]{2,1,0:T(8,128)S(1)}, f32[2,384,128]{2,1,0:T(8,128)S(1)}, u32[]{:S(2)}, u32[]{:S(2)}) collective-permute-start(f32[2,384,128]{2,1,0:T(8,128)S(1)} %get-tuple-element.23), channel_id=1, source_target_pairs={{0,1},{1,2},{2,3},{3,4},{4,5},{5,6},{6,7},{7,8},{8,9},{9,10},{10,1... | collective-permute-start | bytes 1179656 | tf_op jit(solution)/shard_map/ppermute | solution.py:293
  95.2 32.1 %collective-permute-start.18 = (f32[2,3,128,128]{3,2,1,0:T(8,128)S(1)}, f32[2,3,128,128]{3,2,1,0:T(8,128)S(1)}, u32[]{:S(2)}, u32[]{:S(2)}) collective-permute-start(f32[2,3,128,128]{3,2,1,0:T(8,128)S(1)} %get-tuple-element.24), channel_id=1, source_target_pairs={{0,224},{1,225},{2,226},{3,227},{4,228},{5,229},{6,230},{7,231},{8... | collective-permute-start | bytes 1179656 | tf_op jit(solution)/shard_map/ppermute | solution.py:293
  98.4 28.9 %collective-permute-start.17 = (f32[2,3,128,128]{3,2,1,0:T(8,128)S(1)}, f32[2,3,128,128]{3,2,1,0:T(8,128)S(1)}, u32[]{:S(2)}, u32[]{:S(2)}) collective-permute-start(f32[2,3,128,128]{3,2,1,0:T(8,128)S(1)} %get-tuple-element.25), channel_id=1, source_target_pairs={{0,32},{1,33},{2,34},{3,35},{4,36},{5,37},{6,38},{7,39},{8,40},{9,... | collective-permute-start | bytes 1179656 | tf_op jit(solution)/shard_map/ppermute | solution.py:293
  98.4 15.7 %collective-permute-start.21 = (f32[2,128,128]{2,1,0:T(8,128)S(1)}, f32[2,128,128]{2,1,0:T(8,128)S(1)}, u32[]{:S(2)}, u32[]{:S(2)}) collective-permute-start(f32[2,128,128]{2,1,0:T(8,128)S(1)} %get-tuple-element.21), channel_id=1, source_target_pairs={{0,33},{1,34},{2,35},{3,36},{4,37},{5,38},{6,39},{7,40},{8,41},{9,... | collective-permute-start | bytes 393224 | tf_op jit(solution)/shard_map/ppermute | solution.py:293
  114.8 18.0 %collective-permute-start.16 = (f32[2,64,128]{2,1,0:T(8,128)S(1)}, f32[2,64,128]{2,1,0:T(8,128)S(1)}, u32[]{:S(2)}, u32[]{:S(2)}) collective-permute-start(f32[2,64,128]{2,1,0:T(8,128)S(1)} %fusion.1), channel_id=1, source_target_pairs={{0,1},{1,0},{2,3},{3,2},{4,5},{5,4},{6,7},{7,6},{8,9},{9,8},{10,11... | collective-permute-start | bytes 196616 | tf_op jit(solution)/shard_map/ppermute | solution.py:301
  172.0 18.1 %collective-permute-start.32 = (f32[2,128,128]{2,1,0:T(8,128)S(1)}, f32[2,128,128]{2,1,0:T(8,128)S(1)}, u32[]{:S(2)}, u32[]{:S(2)}) collective-permute-start(f32[2,128,128]{2,1,0:T(8,128)S(1)} %get-tuple-element.10), channel_id=1, source_target_pairs={{0,255},{1,224},{2,225},{3,226},{4,227},{5,228},{6,229},{7,230},{8... | collective-permute-start | bytes 393224 | tf_op jit(solution)/shard_map/ppermute | solution.py:293
  174.5 15.8 %collective-permute-start.31 = (f32[2,128,128]{2,1,0:T(8,128)S(1)}, f32[2,128,128]{2,1,0:T(8,128)S(1)}, u32[]{:S(2)}, u32[]{:S(2)}) collective-permute-start(f32[2,128,128]{2,1,0:T(8,128)S(1)} %get-tuple-element.11), channel_id=1, source_target_pairs={{0,225},{1,226},{2,227},{3,228},{4,229},{5,230},{6,231},{7,232},{8... | collective-permute-start | bytes 393224 | tf_op jit(solution)/shard_map/ppermute | solution.py:293
  176.9 14.8 %collective-permute-start.30 = (f32[2,128,128]{2,1,0:T(8,128)S(1)}, f32[2,128,128]{2,1,0:T(8,128)S(1)}, u32[]{:S(2)}, u32[]{:S(2)}) collective-permute-start(f32[2,128,128]{2,1,0:T(8,128)S(1)} %get-tuple-element.12), channel_id=1, source_target_pairs={{0,63},{1,32},{2,33},{3,34},{4,35},{5,36},{6,37},{7,38},{8,39},{9,... | collective-permute-start | bytes 393224 | tf_op jit(solution)/shard_map/ppermute | solution.py:293
  182.6 37.4 %collective-permute-start.28 = (f32[2,384,128]{2,1,0:T(8,128)S(1)}, f32[2,384,128]{2,1,0:T(8,128)S(1)}, u32[]{:S(2)}, u32[]{:S(2)}) collective-permute-start(f32[2,384,128]{2,1,0:T(8,128)S(1)} %get-tuple-element.14), channel_id=1, source_target_pairs={{0,31},{1,0},{2,1},{3,2},{4,3},{5,4},{6,5},{7,6},{8,7},{9,8},{10,9... | collective-permute-start | bytes 1179656 | tf_op jit(solution)/shard_map/ppermute | solution.py:293
  186.4 33.6 %collective-permute-start.27 = (f32[2,384,128]{2,1,0:T(8,128)S(1)}, f32[2,384,128]{2,1,0:T(8,128)S(1)}, u32[]{:S(2)}, u32[]{:S(2)}) collective-permute-start(f32[2,384,128]{2,1,0:T(8,128)S(1)} %get-tuple-element.15), channel_id=1, source_target_pairs={{0,1},{1,2},{2,3},{3,4},{4,5},{5,6},{6,7},{7,8},{8,9},{9,10},{10,1... | collective-permute-start | bytes 1179656 | tf_op jit(solution)/shard_map/ppermute | solution.py:293
  190.1 29.9 %collective-permute-start.26 = (f32[2,3,128,128]{3,2,1,0:T(8,128)S(1)}, f32[2,3,128,128]{3,2,1,0:T(8,128)S(1)}, u32[]{:S(2)}, u32[]{:S(2)}) collective-permute-start(f32[2,3,128,128]{3,2,1,0:T(8,128)S(1)} %get-tuple-element.16), channel_id=1, source_target_pairs={{0,224},{1,225},{2,226},{3,227},{4,228},{5,229},{6,230},{7,231},{8... | collective-permute-start | bytes 1179656 | tf_op jit(solution)/shard_map/ppermute | solution.py:293
  190.3 29.7 %collective-permute-start.25 = (f32[2,3,128,128]{3,2,1,0:T(8,128)S(1)}, f32[2,3,128,128]{3,2,1,0:T(8,128)S(1)}, u32[]{:S(2)}, u32[]{:S(2)}) collective-permute-start(f32[2,3,128,128]{3,2,1,0:T(8,128)S(1)} %get-tuple-element.17), channel_id=1, source_target_pairs={{0,32},{1,33},{2,34},{3,35},{4,36},{5,37},{6,38},{7,39},{8,40},{9,... | collective-permute-start | bytes 1179656 | tf_op jit(solution)/shard_map/ppermute | solution.py:293
  191.7 14.4 %collective-permute-start.29 = (f32[2,128,128]{2,1,0:T(8,128)S(1)}, f32[2,128,128]{2,1,0:T(8,128)S(1)}, u32[]{:S(2)}, u32[]{:S(2)}) collective-permute-start(f32[2,128,128]{2,1,0:T(8,128)S(1)} %get-tuple-element.13), channel_id=1, source_target_pairs={{0,33},{1,34},{2,35},{3,36},{4,37},{5,38},{6,39},{7,40},{8,41},{9,... | collective-permute-start | bytes 393224 | tf_op jit(solution)/shard_map/ppermute | solution.py:293
  206.1 19.2 %collective-permute-start.41 = (f32[2,64,128]{2,1,0:T(8,128)S(1)}, f32[2,64,128]{2,1,0:T(8,128)S(1)}, u32[]{:S(2)}, u32[]{:S(2)}) collective-permute-start(f32[2,64,128]{2,1,0:T(8,128)S(1)} %fusion), channel_id=1, source_target_pairs={{0,1},{1,0},{2,3},{3,2},{4,5},{5,4},{6,7},{7,6},{8,9},{9,8},{10,11... | collective-permute-start | bytes 196616 | tf_op jit(solution)/shard_map/ppermute | solution.py:301
  (49 other events, 421.1 us)

commit v2 on v0

v2 whole, which is shorter than its diff:
```python
import functools
import math

import jax
import jax.numpy as jnp
from jax import lax
from jax.experimental import pallas as pl
from jax.experimental.pallas import tpu as pltpu
from jax.sharding import PartitionSpec as P

WIDTH = 128
RIM = WIDTH // 2
TILE = 256
EXT = TILE + WIDTH
BLOCKS = EXT // WIDTH
GROUP = 4
CHAINS = 2
VMEM_LIMIT = 16 * 1024 * 1024


def split(value):
    high = value.astype(jnp.bfloat16)
    low = (value - high.astype(jnp.float32)).astype(jnp.bfloat16)
    return high, low


def times_right(value, table):
    high, low = split(value)
    return jnp.dot(
        jnp.concatenate([high, low, high], 1), table, preferred_element_type=jnp.float32
    )


def times_left(table, value):
    high, low = split(value)
    return jnp.dot(
        table, jnp.concatenate([high, low, high], 0), preferred_element_type=jnp.float32
    )


def columns_to_rows(value):
    count = value.shape[0] // WIDTH
    parts = [value[i * WIDTH : (i + 1) * WIDTH] for i in range(count)]
    return jnp.concatenate(
        [
            jnp.concatenate([part[:, :WIDTH] for part in parts], 1),
            jnp.concatenate([part[:, WIDTH:] for part in parts], 1),
        ],
        0,
    )


def rows_to_columns(value):
    count = value.shape[1] // WIDTH
    cut = [value[:, i * WIDTH : (i + 1) * WIDTH] for i in range(count)]
    return jnp.concatenate(
        [jnp.concatenate([part[:WIDTH], part[WIDTH:]], 1) for part in cut], 0
    )


def gate(value, *conditions):
    for condition in conditions:
        value = jnp.where(condition, value, 0.0)
    return value


def half_turn(value):
    return pltpu.roll(value, RIM, 1)


def lane_of(rows):
    return lax.broadcasted_iota(jnp.int32, (rows, WIDTH), 1)


def plan_kernel(flags_ref, slots_ref):
    iterations, cap = flags_ref.shape
    for step in range(iterations):

        def note(slot, count):
            live = flags_ref[step, slot] != 0

            @pl.when(live)
            def _():
                slots_ref[step, count] = slot

            return count + live.astype(jnp.int32)

        slots_ref[step, cap] = lax.fori_loop(0, cap, note, jnp.int32(0))


def prepare_kernel(after_ref, amp_ref, probe_ref, ra_ref, lb_ref, la_ref, rb_ref, amp_out, probe_out):
    down = lax.broadcasted_iota(jnp.int32, (WIDTH, WIDTH), 0)
    along = lax.broadcasted_iota(jnp.int32, (WIDTH, WIDTH), 1)
    angle = (down * along % WIDTH).astype(jnp.float32) * (2.0 * math.pi / WIDTH)
    cos_t = jnp.cos(angle) * (1.0 / math.sqrt(WIDTH))
    sin_t = jnp.sin(angle) * (1.0 / math.sqrt(WIDTH))
    cos_h, cos_l = split(cos_t)
    sin_h, sin_l = split(sin_t)
    begin, end = pl.ds(0, WIDTH), pl.ds(WIDTH, WIDTH)
    for place, (cos_p, sin_p) in enumerate(((cos_h, sin_h), (cos_h, sin_h), (cos_l, sin_l))):
        first, second = pl.ds(2 * place * WIDTH, WIDTH), pl.ds((2 * place + 1) * WIDTH, WIDTH)
        for right, left, sign in ((ra_ref, la_ref, 1), (rb_ref, lb_ref, -1)):
            upper, lower = (-sin_p, sin_p) if sign > 0 else (sin_p, -sin_p)
            right[first, begin] = cos_p
            right[first, end] = upper
            right[second, begin] = lower
            right[second, end] = cos_p
            left[begin, first] = cos_p
            left[begin, second] = upper
            left[end, first] = lower
            left[end, second] = cos_p
    amp_out[...] = amp_ref[...]
    probe_out[...] = probe_ref[...]


def pack_kernel(obj_ref, down_ref, up_ref, east_ref, west_ref):
    low = lane_of(WIDTH) < RIM
    up_ref[...] = obj_ref[:, pl.ds(0, RIM), :]
    down_ref[...] = obj_ref[:, pl.ds(TILE - RIM, RIM), :]
    top, bottom = pl.ds(0, WIDTH), pl.ds(WIDTH, WIDTH)
    begin, end = pl.ds(0, WIDTH), pl.ds(TILE - WIDTH, WIDTH)
    for part in range(2):
        west_ref[part] = jnp.where(
            low, obj_ref[part, top, begin], half_turn(obj_ref[part, bottom, begin])
        )
        east_ref[part] = jnp.where(
            low, half_turn(obj_ref[part, top, end]), obj_ref[part, bottom, end]
        )


def corners_kernel(where_ref, up, down, east_ref, west_ref, after_ref):
    after_ref[...] = jnp.zeros_like(after_ref)
    has_up, has_down = where_ref[0] != 0, where_ref[1] != 0
    low = lane_of(RIM) < RIM
    for part in range(2):
        above, below = gate(up[part], has_up), gate(down[part], has_down)
        west_ref[part] = jnp.where(low, above[:, :WIDTH], half_turn(below[:, :WIDTH]))
        east_ref[part] = jnp.where(low, half_turn(above[:, WIDTH:]), below[:, WIDTH:])


def assemble(where_ref, obj_ref, up, down, from_left, from_right, corner_left, corner_right, ext_ref):
    has = [where_ref[i] != 0 for i in range(4)]
    low = lane_of(RIM) < RIM
    for part in range(2):
        for step in range(EXT // RIM):
            rows = pl.ds(step * RIM, RIM)
            if step == 0:
                mid = gate(up[part], has[0])
                left, right = corner_left[part], half_turn(corner_right[part])
            elif step == EXT // RIM - 1:
                mid = gate(down[part], has[1])
                left, right = half_turn(corner_left[part]), corner_right[part]
            else:
                mid = obj_ref[part, pl.ds((step - 1) * RIM, RIM), :]
                at = pl.ds((step - 1) % 2 * RIM, RIM)
                left, right = from_left[part, at, :], from_right[part, at, :]
                if step <= 2:
                    right = half_turn(right)
                else:
                    left = half_turn(left)
            first, second = half_turn(mid[:, :WIDTH]), half_turn(mid[:, WIDTH:])
            ext_ref[part, 0, rows, :] = jnp.where(low, gate(left, has[2]), first)
            ext_ref[part, 1, rows, :] = jnp.where(low, first, second)
            ext_ref[part, 2, rows, :] = jnp.where(low, second, gate(right, has[3]))


def patterns_kernel(first, last, *refs):
    (slots_ref, rows_ref, cols_ref, where_ref), refs = refs[:4], refs[4:]
    cap = rows_ref.shape[0]
    if first:
        (amp_ref, ra_ref, lb_ref, la_ref, rb_ref), halo, refs = refs[:5], refs[5:12], refs[12:]
        probe_ref, refs = refs[0], refs[1:]
        (acc_ref, east_ref, west_ref, mine_ref, other_ref, held_ref, ext_ref, sums_ref) = refs
        assemble(where_ref, *halo, ext_ref)
    else:
        (amp_ref, ra_ref, lb_ref, la_ref, rb_ref), refs = refs[:5], refs[5:]
        (ext_ref, held_mine, held_other), refs = refs[:3], refs[3:]
        (acc_ref, east_ref, west_ref, mine_ref, other_ref, held_ref, probe_ref, sums_ref) = refs
        here = pl.multiple_of(where_ref[4] * RIM, RIM)
        there = pl.multiple_of((1 - where_ref[4]) * RIM, RIM)
        probe_ref[:, pl.ds(here, RIM), :] = held_mine[...]
        probe_ref[:, pl.ds(there, RIM), :] = held_other[...]
    count = slots_ref[cap]
    acc_ref[...] = jnp.zeros_like(acc_ref)
    sums_ref[...] = jnp.zeros_like(sums_ref)
    lane = lane_of(WIDTH)

    def where_is(slot):
        left = cols_ref[slot]
        block = left // WIDTH
        return rows_ref[slot], block, left - block * WIDTH

    def patch(slot):
        top, block, shift = where_is(slot)
        parts = []
        for part in range(2):
            near = ext_ref[part, block, pl.ds(top, WIDTH), :]
            far = ext_ref[part, block + 1, pl.ds(top, WIDTH), :]
            merged = jnp.where(lane >= shift, near, far)
            parts.append(pltpu.roll(merged, (WIDTH - shift) % WIDTH, 1))
        return parts

    def place(slot, update):
        top, block, shift = where_is(slot)
        for part in range(2):
            rolled = pltpu.roll(update[part], shift, 1)
            acc_ref[part, block, pl.ds(top, WIDTH), :] += jnp.where(lane >= shift, rolled, 0.0)
            acc_ref[part, block + 1, pl.ds(top, WIDTH), :] += jnp.where(lane < shift, rolled, 0.0)

    def several(base):
        chosen = [slots_ref[jnp.minimum(base + i, count - 1)] for i in range(GROUP)]
        keep = [(base + i < count).astype(jnp.float32) for i in range(GROUP)]
        pr, pi = probe_ref[0], probe_ref[1]
        waves = []
        objs = []
        for slot in chosen:
            obj_re, obj_im = patch(slot)
            objs.append((obj_re, obj_im))
            waves.append(
                jnp.concatenate([pr * obj_re - pi * obj_im, pr * obj_im + pi * obj_re], 1)
            )
        field = times_right(jnp.concatenate(waves, 0), ra_ref[...])
        field = times_left(lb_ref[...], columns_to_rows(field))
        big_re, big_im = field[:WIDTH], field[WIDTH:]
        inverse = jnp.minimum(lax.rsqrt(big_re * big_re + big_im * big_im), 2.0)
        factor = []
        for which, slot in enumerate(chosen):
            amp = amp_ref[slot].astype(jnp.float32)
            part = inverse[:, which * WIDTH : (which + 1) * WIDTH]
            factor.append((1.0 - amp * part) * keep[which])
        factor = jnp.concatenate(factor, 1)
        chi = jnp.concatenate([big_re * factor, big_im * factor], 0)
        field = times_left(la_ref[...], chi)
        field = times_right(rows_to_columns(field), rb_ref[...])
        grad_re = grad_im = weight = jnp.zeros((WIDTH, WIDTH), jnp.float32)
        for which, slot in enumerate(chosen):
            part = field[which * WIDTH : (which + 1) * WIDTH]
            back_re, back_im = part[:, :WIDTH], part[:, WIDTH:]
            obj_re, obj_im = objs[which]
            place(slot, (pr * back_re + pi * back_im, pr * back_im - pi * back_re))
            grad_re = grad_re + (obj_re * back_re + obj_im * back_im)
            grad_im = grad_im + (obj_re * back_im - obj_im * back_re)
            weight = weight + keep[which] * (obj_re * obj_re + obj_im * obj_im)
        sums_ref[0] += grad_re
        sums_ref[1] += grad_im
        sums_ref[2] += weight

    def chains(index, carry):
        for chain in range(CHAINS):
            several((index * CHAINS + chain) * GROUP)
        return carry

    lax.fori_loop(0, (count + CHAINS * GROUP - 1) // (CHAINS * GROUP), chains, jnp.int32(0))

    here = pl.multiple_of(where_ref[4] * RIM, RIM)
    there = pl.multiple_of((1 - where_ref[4]) * RIM, RIM)
    mine_ref[...] = sums_ref[:, pl.ds(here, RIM), :]
    other_ref[...] = sums_ref[:, pl.ds(there, RIM), :]
    held_ref[...] = probe_ref[:, pl.ds(here, RIM), :]
    if last:
        low = lane_of(EXT // 2) < RIM
        top, bottom = pl.ds(0, EXT // 2), pl.ds(EXT // 2, EXT // 2)
        for part in range(2):
            west_ref[part] = jnp.where(
                low, acc_ref[part, 0, top, :], half_turn(acc_ref[part, 0, bottom, :])
            )
            east_ref[part] = jnp.where(
                low, half_turn(acc_ref[part, 2, top, :]), acc_ref[part, 2, bottom, :]
            )
    else:
        west_ref[...] = acc_ref[:, 0]
        east_ref[...] = acc_ref[:, 2]


def fold_kernel(last, where_ref, acc_in, from_left, from_right, acc_ref, down_ref, up_ref, token_ref):
    token_ref[...] = jnp.zeros_like(token_ref)
    has_left, has_right = where_ref[2] != 0, where_ref[3] != 0
    low = lane_of(EXT // 2) < RIM
    for part in range(2):
        acc_ref[part, 1] = acc_in[part, 1]
        left = gate(from_left[part], has_left)
        right = gate(from_right[part], has_right)
        if last:
            for half in range(2):
                rows = pl.ds(half * (EXT // 2), EXT // 2)
                acc_ref[part, 0, rows, :] = acc_in[part, 0, rows, :] + jnp.where(
                    low, 0.0, left if half else half_turn(left)
                )
                acc_ref[part, 2, rows, :] = acc_in[part, 2, rows, :] + jnp.where(
                    low, half_turn(right) if half else right, 0.0
                )
        else:
            acc_ref[part, 0] = acc_in[part, 0] + left
            acc_ref[part, 2] = acc_in[part, 2] + right
    size = down_ref.shape[2]
    up_ref[...] = acc_ref[:, :, pl.ds(0, size), :]
    down_ref[...] = acc_ref[:, :, pl.ds(EXT - size, size), :]


def peak_scale(probe_ref):
    pr, pi = probe_ref[0], probe_ref[1]
    return 1.0 / (jnp.max(pr * pr + pi * pi) + 1e-06)


def update_kernel(where_ref, probe_ref, ext_ref, acc_ref, up, down, out_ref, token_ref):
    token_ref[...] = jnp.zeros_like(token_ref)
    has = [where_ref[i] != 0 for i in range(4)]
    scale = peak_scale(probe_ref)
    upper = lax.broadcasted_iota(jnp.int32, (WIDTH, WIDTH), 0) < RIM
    west = lane_of(WIDTH) < RIM
    for part in range(2):
        for br in range(3):
            for bc in range(3):
                rows = pl.ds(br * WIDTH, WIDTH)
                total = acc_ref[part, bc, rows, :]
                if br == 0:
                    total = total + gate(up[part, bc], has[0])
                if br == 2:
                    total = total + gate(down[part, bc], has[1])
                value = ext_ref[part, bc, rows, :] - total * scale
                if br != 1:
                    value = gate(value, jnp.logical_or(has[br // 2], (~upper) if br == 0 else upper))
                if bc != 1:
                    value = gate(value, jnp.logical_or(has[2 + bc // 2], (~west) if bc == 0 else west))
                out_ref[part, bc, rows, :] = value


def finish_kernel(where_ref, probe_ref, ext_ref, acc_ref, up, down, out_ref, token_ref):
    token_ref[...] = jnp.zeros_like(token_ref)
    has_up, has_down = where_ref[0] != 0, where_ref[1] != 0
    scale = peak_scale(probe_ref)
    west = lane_of(RIM) < RIM
    for part in range(2):
        for step in range(TILE // RIM):
            rows = pl.ds(RIM + step * RIM, RIM)
            turned = []
            for bc in range(3):
                total = acc_ref[part, bc, rows, :]
                if step == 0:
                    total = total + gate(up[part, bc], has_up)
                if step == TILE // RIM - 1:
                    total = total + gate(down[part, bc], has_down)
                turned.append(half_turn(ext_ref[part, bc, rows, :] - total * scale))
            for half in range(2):
                out_ref[part, pl.ds(step * RIM, RIM), pl.ds(half * WIDTH, WIDTH)] = jnp.where(
                    west, turned[half], turned[half + 1]
                )


def local_call(kernel, name, scalars, arrays, outs, scratch=(), scalar_outs=0):
    smem = pl.BlockSpec(memory_space=pltpu.SMEM)
    vmem = pl.BlockSpec(memory_space=pltpu.VMEM)
    shapes = tuple(
        out if isinstance(out, jax.ShapeDtypeStruct) else jax.ShapeDtypeStruct(out, jnp.float32)
        for out in outs
    )
    return pl.pallas_call(
        kernel,
        out_shape=shapes,
        in_specs=[smem] * len(scalars) + [vmem] * len(arrays),
        out_specs=tuple([smem] * scalar_outs + [vmem] * (len(outs) - scalar_outs)),
        scratch_shapes=list(scratch),
        compiler_params=pltpu.CompilerParams(vmem_limit_bytes=VMEM_LIMIT),
        name=name,
    )(*scalars, *arrays)


def on_device(rows_n, cols_n, obj, probe, amplitudes, centres, members):
    def shift(value, down, right):
        pairs = [
            (r * cols_n + c, (r + down) % rows_n * cols_n + (c + right) % cols_n)
            for r in range(rows_n)
            for c in range(cols_n)
        ]
        return lax.ppermute(value, ("row", "col"), pairs)

    def swap(value, *bits):
        pairs = [
            (r * cols_n + c, (r ^ bits[c % 2][0]) * cols_n + (c ^ bits[c % 2][1]))
            for r in range(rows_n)
            for c in range(cols_n)
        ]
        return lax.ppermute(value, ("row", "col"), pairs)

    x_steps = ((1, 0), (3, 0))
    y_steps = ((0, 2), (0, 6))
    z_steps = ((4, 0), (0, 8), (4, 24))
    ladder = tuple(zip(x_steps + y_steps + z_steps, z_steps + y_steps + x_steps))
    twin = ((0, 1), (0, 1))
    iterations, cap = members.shape[0], members.shape[3]
    rows = centres[0, 0, 0]
    cols = centres[1, 0, 0]
    row, col = lax.axis_index("row"), lax.axis_index("col")
    where = jnp.stack(
        [row > 0, row < rows_n - 1, col > 0, col < cols_n - 1, col % 2 == 1]
    ).astype(jnp.int32)
    ext_shape = (2, BLOCKS, EXT, WIDTH)
    strip = (2, RIM, TILE)
    block = (2, WIDTH, WIDTH)
    corner = (2, RIM, WIDTH)
    to_down, to_up, east, west = local_call(
        pack_kernel, "pack", (), (obj,), (strip, strip, block, block)
    )
    up, down = shift(to_down, 1, 0), shift(to_up, -1, 0)
    from_left, from_right = shift(east, 0, 1), shift(west, 0, -1)
    (slots,) = local_call(
        plan_kernel, "plan", (members[:, 0, 0],), (),
        (jax.ShapeDtypeStruct((iterations, cap + 1), jnp.int32),), scalar_outs=1,
    )
    east, west, after = local_call(
        corners_kernel, "corners", (where,), (up, down), (corner, corner, (8, WIDTH))
    )
    amp = amplitudes[0, 0]
    tall = jax.ShapeDtypeStruct((6 * WIDTH, 2 * WIDTH), jnp.bfloat16)
    wide = jax.ShapeDtypeStruct((2 * WIDTH, 6 * WIDTH), jnp.bfloat16)
    *tables, amp, probe = local_call(
        prepare_kernel, "prepare", (), (after, amp, probe),
        (tall, wide, wide, tall, jax.ShapeDtypeStruct(amp.shape, amp.dtype), block),
    )
    kept = (amp, *tables)
    halo = (obj, up, down, from_left, from_right, shift(east, 0, 1), shift(west, 0, -1))
    halves = None
    ext = None
    sums_scratch = (pltpu.VMEM((3, WIDTH, WIDTH), jnp.float32),)
    for step in range(iterations):
        first, last = step == 0, step == iterations - 1
        size = RIM if last else WIDTH
        strip = (2, EXT // 2, WIDTH) if last else (2, EXT, WIDTH)
        outs = (ext_shape, strip, strip) + ((3, RIM, WIDTH),) * 2 + (corner,)
        kernel = functools.partial(patterns_kernel, first, last)
        scalars = (slots[step], rows, cols, where)
        if first:
            acc, east, west, mine, other, held, ext = local_call(
                kernel, "patterns", scalars, (*kept, *halo, probe), outs + (ext_shape,), sums_scratch
            )
        else:
            acc, east, west, mine, other, held, probe = local_call(
                kernel, "patterns", scalars, (*kept, ext, *halves),
                outs + (block,), sums_scratch,
            )
        from_left = shift(east, 0, 1)
        from_right = shift(west, 0, -1)
        total = mine + swap(other, *twin)
        total = total + swap(total, *ladder[0])
        total = total + swap(total, *ladder[1])
        acc, to_down, to_up, token = local_call(
            functools.partial(fold_kernel, last), "fold", (where,), (acc, from_left, from_right),
            (ext_shape,) + ((2, BLOCKS, size, WIDTH),) * 2 + ((RIM, WIDTH),),
        )
        up = shift(to_down, 1, 0)
        down = shift(to_up, -1, 0)
        total = total + swap(total, *ladder[2]) + token
        total = total + swap(total, *ladder[3])
        total = total + swap(total, *ladder[4])
        total = total + swap(total, *ladder[5])
        ext, token = local_call(
            finish_kernel if last else update_kernel, "finish" if last else "update", (where,),
            (probe, ext, acc, up, down), (obj.shape if last else ext_shape, (RIM, WIDTH)),
        )
        total = total + swap(total, *ladder[6]) + token
        held = held - total[:2] / (total[2] + 1e-06)
        halves = (held, swap(held, *twin))
    held, other = halves
    probe = jnp.where(
        col % 2 == 0, jnp.concatenate([held, other], 1), jnp.concatenate([other, held], 1)
    )
    return ext, probe


def solution(mesh):
    in_specs = (
        P(None, "row", "col"),
        P(),
        P("row", "col", None, None, None),
        P(None, "row", "col", None),
        P(None, "row", "col", None),
    )
    out_specs = (P(None, "row", "col"), P())
    body = functools.partial(on_device, mesh.shape["row"], mesh.shape["col"])
    return jax.shard_map(
        body, mesh=mesh, in_specs=in_specs, out_specs=out_specs, check_vma=False
    )
```

time: 1420 us -> 138 us (0.10); the launches traced: 1400 us -> 138 us
  waiting for transfers between devices: 518 us -> 39.3 us
  local copies, waits for them, and re-layouts: 415 us -> 4.63 us
  loops' own time: 251 us -> 0 us
  other arithmetic: 95.1 us -> 0.94 us
  matrix products: 53.3 us -> 0 us
  Pallas kernels: 0 us -> 22 us
  starting transfers between devices: 53.2 us -> 69.8 us
  between operations: 16.4 us -> 0.93 us
    psum x2 -> x0, waiting for transfers between devices: 493 us -> none  [on_device(): grad_sum, weight_sum = lax.psum((grad_p, weight_p), ('row', 'col'))]
    another operation x4 -> x0, loops' own time: 251 us -> none  [the longest x2 251 us: on_device(): acc = lax.fori_loop(0, update.shape[0], place, jnp.zeros_like(extended))]
    gather x192 -> x0, local copies, waits for them, and re-layouts: 168 us -> none
    dynamic_update_slice x64 -> x0, local copies, waits for them, and re-layouts: 156 us -> none  [place(): return lax.dynamic_update_slice(acc, current + update[slot], start)]
    dynamic_slice x128 -> x0, local copies, waits for them, and re-layouts: 75.2 us -> none  [place(): start = (0, rows_all[slot], cols_all[slot])]
    add x70 -> x16, other arithmetic: 68.8 us -> 0.22 us  [the longest x2 0.03 us: on_device(): total = total + swap(total, *ladder[0])]
    dot_general x12 -> x0, matrix products: 53.3 us -> none  [the longest x4 18.7 us: transform(): with_cos = jnp.einsum('jr,brk->bjk', cos_t, field, precision=HIGH)]
    pallas_call x0 -> x10, Pallas kernels: none -> 22 us  [local_call(): pl.pallas_call(kernel, out_shape=shapes, in_specs=[smem] * len(scalars) +...]
  transfers between devices with their start and end apart: 18 -> 32, of which waited for: 11 -> 17; matrix products, arithmetic and copies ran while one was open for 1% -> 1% of each run, Pallas kernels for 0% -> 5%
where the time goes in v2:
time: 138 us
  starting transfers between devices  69.8 us (51%)
  waiting for transfers between devices  39.3 us (28%)
  Pallas kernels  22 us (16%)
  local copies, waits for them, and re-layouts  4.63 us (3%)
    ppermute x18, starting transfers between devices, swap(): return lax.ppermute(value, ('row', 'col'), pairs)  49.7 us
    ppermute x18, waiting for transfers between devices, swap(): return lax.ppermute(value, ('row', 'col'), pairs)  39.3 us
    pallas_call x10, Pallas kernels, local_call(): pl.pallas_call(kernel, out_shape=shapes, in_specs=[smem] * len(scalars) +...  22 us
    ppermute x14, starting transfers between devices, shift(): return lax.ppermute(value, ('row', 'col'), pairs)  20.1 us
    unnamed x10, local copies, waits for them, and re-layouts  3.85 us
  transfers between devices with their start and end apart: 32, of which 17 were waited for; matrix products, arithmetic and copies ran while one was open for 1% of the time, Pallas kernels for 5%

profile of v2, /device:TPU:33, one launch (start us, length us, event | category | flops | bytes accessed | tf_op | source)
XLA Modules:
  0.0 137.6 jit_solution(6186873612183395313)
XLA Ops:
  3.1 2.4 %collective-permute-start.1 = (f32[2,64,256]{2,1,0:T(8,128)S(1)}, f32[2,64,256]{2,1,0:T(8,128)S(1)}, u32[]{:S(2)}, u32[]{:S(2)}) collective-permute-start(f32[2,64,256]{2,1,0:T(8,128)S(1)} %get-tuple-element.42), channel_id=1, source_target_pairs={{0,224},{1,225},{2,226},{3,227},{4,228},{5,229},{6,230},{7,231},{8... | collective-permute-start | bytes 393224 | tf_op jit(solution)/shard_map/ppermute | solution.py:375
  5.5 2.4 %collective-permute-start.2 = (f32[2,128,128]{2,1,0:T(8,128)S(1)}, f32[2,128,128]{2,1,0:T(8,128)S(1)}, u32[]{:S(2)}, u32[]{:S(2)}) collective-permute-start(f32[2,128,128]{2,1,0:T(8,128)S(1)} %get-tuple-element.50), channel_id=1, source_target_pairs={{0,1},{1,2},{2,3},{3,4},{4,5},{5,6},{6,7},{7,8},{8,9},{9,10},{10,1... | collective-permute-start | bytes 393224 | tf_op jit(solution)/shard_map/ppermute | solution.py:375
  13.1 3.9 %collective-permute-start.5 = (f32[2,64,128]{2,1,0:T(8,128)S(1)}, f32[2,64,128]{2,1,0:T(8,128)S(1)}, u32[]{:S(2)}, u32[]{:S(2)}) collective-permute-start(f32[2,64,128]{2,1,0:T(8,128)S(1)} %get-tuple-element.53), channel_id=1, source_target_pairs={{0,31},{1,0},{2,1},{3,2},{4,3},{5,4},{6,5},{7,6},{8,7},{9,8},{10,9... | collective-permute-start | bytes 196616 | tf_op jit(solution)/shard_map/ppermute | solution.py:375
  20.3 7.5 %patterns.2 = (f32[2,3,384,128]{3,2,1,0:T(8,128)S(1)}, f32[2,384,128]{2,1,0:T(8,128)S(1)}, f32[2,384,128]{2,1,0:T(8,128)S(1)}, f32[3,64,128]{2,1,0:T(8,128)S(1)}...) custom-call(s32[33]{0:T(128)S(1)} %get-tuple-element.80.refs_0_, ...), custom_call_target="tpu_custom_call" | custom-call | tf_op jit(solution)/shard_map/patterns/pallas_call | solution.py:357
  27.8 2.7 %collective-permute-start.10 = (f32[3,64,128]{2,1,0:T(8,128)S(1)}, f32[3,64,128]{2,1,0:T(8,128)S(1)}, u32[]{:S(2)}, u32[]{:S(2)}) collective-permute-start(f32[3,64,128]{2,1,0:T(8,128)S(1)} %get-tuple-element.64), channel_id=1, source_target_pairs={{0,1},{1,0},{2,3},{3,2},{4,5},{5,4},{6,7},{7,6},{8,9},{9,8},{10,11... | collective-permute-start | bytes 294920 | tf_op jit(solution)/shard_map/ppermute | solution.py:383
  31.5 4.0 %collective-permute-start.11 = (f32[3,64,128]{2,1,0:T(8,128)S(1)}, f32[3,64,128]{2,1,0:T(8,128)S(1)}, u32[]{:S(2)}, u32[]{:S(2)}) collective-permute-start(f32[3,64,128]{2,1,0:T(8,128)S(1)} %add.94), channel_id=1, source_target_pairs={{0,32},{1,129},{2,34},{3,131},{4,36},{5,133},{6,38},{7,135},{8,40}... | collective-permute-start | bytes 294920 | tf_op jit(solution)/shard_map/ppermute | solution.py:383
  37.7 4.6 %collective-permute-done.12 = f32[3,64,128]{2,1,0:T(8,128)S(1)} collective-permute-done((f32[3,64,128]{2,1,0:T(8,128)S(1)}, f32[3,64,128]{2,1,0:T(8,128)S(1)}, u32[]{:S(2)}, u32[]{:S(2)}) %collective-permute-start.12) | collective-permute-done | bytes 98336 | tf_op jit(solution)/shard_map/ppermute | solution.py:383
  42.3 5.7 %collective-permute-start.13 = (f32[3,64,128]{2,1,0:T(8,128)S(1)}, f32[3,64,128]{2,1,0:T(8,128)S(1)}, u32[]{:S(2)}, u32[]{:S(2)}) collective-permute-start(f32[3,64,128]{2,1,0:T(8,128)S(1)} %add.96), channel_id=1, source_target_pairs={{0,2},{1,153},{2,0},{3,155},{4,6},{5,157},{6,4},{7,159},{8,10},{9,... | collective-permute-start | bytes 294920 | tf_op jit(solution)/shard_map/ppermute | solution.py:383
  51.1 2.7 %collective-permute-start.9 = (f32[2,3,128,128]{3,2,1,0:T(8,128)S(1)}, f32[2,3,128,128]{3,2,1,0:T(8,128)S(1)}, u32[]{:S(2)}, u32[]{:S(2)}) collective-permute-start(f32[2,3,128,128]{3,2,1,0:T(8,128)S(1)} %get-tuple-element.60), channel_id=1, source_target_pairs={{0,224},{1,225},{2,226},{3,227},{4,228},{5,229},{6,230},{7,231},{8... | collective-permute-start | bytes 1179656 | tf_op jit(solution)/shard_map/ppermute | solution.py:375
  54.8 6.0 %collective-permute-start.15 = (f32[3,64,128]{2,1,0:T(8,128)S(1)}, f32[3,64,128]{2,1,0:T(8,128)S(1)}, u32[]{:S(2)}, u32[]{:S(2)}) collective-permute-start(f32[3,64,128]{2,1,0:T(8,128)S(1)} %add.100), channel_id=1, source_target_pairs={{0,128},{1,7},{2,130},{3,5},{4,132},{5,3},{6,134},{7,1},{8,136},{9... | collective-permute-start | bytes 294920 | tf_op jit(solution)/shard_map/ppermute | solution.py:383
  63.9 3.1 %collective-permute-done.16 = f32[3,64,128]{2,1,0:T(8,128)S(1)} collective-permute-done((f32[3,64,128]{2,1,0:T(8,128)S(1)}, f32[3,64,128]{2,1,0:T(8,128)S(1)}, u32[]{:S(2)}, u32[]{:S(2)}) %collective-permute-start.16) | collective-permute-done | bytes 98336 | tf_op jit(solution)/shard_map/ppermute | solution.py:383
  67.0 3.3 %collective-permute-start.17 = (f32[3,64,128]{2,1,0:T(8,128)S(1)}, f32[3,64,128]{2,1,0:T(8,128)S(1)}, u32[]{:S(2)}, u32[]{:S(2)}) collective-permute-start(f32[3,64,128]{2,1,0:T(8,128)S(1)} %add.102), channel_id=1, source_target_pairs={{0,152},{1,97},{2,154},{3,99},{4,156},{5,101},{6,158},{7,103},{8,1... | collective-permute-start | bytes 294920 | tf_op jit(solution)/shard_map/ppermute | solution.py:383
  72.3 11.5 %collective-permute-start.18 = (f32[2,64,128]{2,1,0:T(8,128)S(1)}, f32[2,64,128]{2,1,0:T(8,128)S(1)}, u32[]{:S(2)}, u32[]{:S(2)}) collective-permute-start(f32[2,64,128]{2,1,0:T(8,128)S(1)} %fusion.1.refs_10_), channel_id=1, source_target_pairs={{0,1},{1,0},{2,3},{3,2},{4,5},{5,4},{6,7},{7,6},{8,9},{9,8},{10,11... | collective-permute-start | bytes 196616 | tf_op jit(solution)/shard_map/ppermute | solution.py:383
  84.8 7.2 %patterns.3 = (f32[2,3,384,128]{3,2,1,0:T(8,128)S(1)}, f32[2,192,128]{2,1,0:T(8,128)S(1)}, f32[2,192,128]{2,1,0:T(8,128)S(1)}, f32[3,64,128]{2,1,0:T(8,128)S(1)}...) custom-call(s32[33]{0:T(128)S(1)} %get-tuple-element.81.refs_0_, ...), custom_call_target="tpu_custom_call" | custom-call | tf_op jit(solution)/shard_map/patterns/pallas_call | solution.py:357
  94.1 3.2 %collective-permute-done.24 = f32[3,64,128]{2,1,0:T(8,128)S(1)} collective-permute-done((f32[3,64,128]{2,1,0:T(8,128)S(1)}, f32[3,64,128]{2,1,0:T(8,128)S(1)}, u32[]{:S(2)}, u32[]{:S(2)}) %collective-permute-start.24) | collective-permute-done | bytes 98336 | tf_op jit(solution)/shard_map/ppermute | solution.py:383
  97.3 2.4 %collective-permute-start.25 = (f32[3,64,128]{2,1,0:T(8,128)S(1)}, f32[3,64,128]{2,1,0:T(8,128)S(1)}, u32[]{:S(2)}, u32[]{:S(2)}) collective-permute-start(f32[3,64,128]{2,1,0:T(8,128)S(1)} %add.108), channel_id=1, source_target_pairs={{0,96},{1,9},{2,98},{3,11},{4,100},{5,13},{6,102},{7,15},{8,104},{... | collective-permute-start | bytes 294920 | tf_op jit(solution)/shard_map/ppermute | solution.py:383
  99.7 2.6 %collective-permute-done.25 = f32[3,64,128]{2,1,0:T(8,128)S(1)} collective-permute-done((f32[3,64,128]{2,1,0:T(8,128)S(1)}, f32[3,64,128]{2,1,0:T(8,128)S(1)}, u32[]{:S(2)}, u32[]{:S(2)}) %collective-permute-start.25) | collective-permute-done | bytes 98336 | tf_op jit(solution)/shard_map/ppermute | solution.py:383
  102.3 3.2 %collective-permute-start.26 = (f32[3,64,128]{2,1,0:T(8,128)S(1)}, f32[3,64,128]{2,1,0:T(8,128)S(1)}, u32[]{:S(2)}, u32[]{:S(2)}) collective-permute-start(f32[3,64,128]{2,1,0:T(8,128)S(1)} %add.109), channel_id=1, source_target_pairs={{0,2},{1,153},{2,0},{3,155},{4,6},{5,157},{6,4},{7,159},{8,10},{9,... | collective-permute-start | bytes 294920 | tf_op jit(solution)/shard_map/ppermute | solution.py:383
  106.2 2.7 %collective-permute-done.26 = f32[3,64,128]{2,1,0:T(8,128)S(1)} collective-permute-done((f32[3,64,128]{2,1,0:T(8,128)S(1)}, f32[3,64,128]{2,1,0:T(8,128)S(1)}, u32[]{:S(2)}, u32[]{:S(2)}) %collective-permute-start.26) | collective-permute-done | bytes 98336 | tf_op jit(solution)/shard_map/ppermute | solution.py:383
  109.1 3.5 %collective-permute-done.27 = f32[3,64,128]{2,1,0:T(8,128)S(1)} collective-permute-done((f32[3,64,128]{2,1,0:T(8,128)S(1)}, f32[3,64,128]{2,1,0:T(8,128)S(1)}, u32[]{:S(2)}, u32[]{:S(2)}) %collective-permute-start.27) | collective-permute-done | bytes 98336 | tf_op jit(solution)/shard_map/ppermute | solution.py:383
  112.5 3.2 %collective-permute-start.28 = (f32[3,64,128]{2,1,0:T(8,128)S(1)}, f32[3,64,128]{2,1,0:T(8,128)S(1)}, u32[]{:S(2)}, u32[]{:S(2)}) collective-permute-start(f32[3,64,128]{2,1,0:T(8,128)S(1)} %add.113), channel_id=1, source_target_pairs={{0,128},{1,7},{2,130},{3,5},{4,132},{5,3},{6,134},{7,1},{8,136},{9... | collective-permute-start | bytes 294920 | tf_op jit(solution)/shard_map/ppermute | solution.py:383
  119.4 5.5 %collective-permute-done.29 = f32[3,64,128]{2,1,0:T(8,128)S(1)} collective-permute-done((f32[3,64,128]{2,1,0:T(8,128)S(1)}, f32[3,64,128]{2,1,0:T(8,128)S(1)}, u32[]{:S(2)}, u32[]{:S(2)}) %collective-permute-start.29) | collective-permute-done | bytes 98336 | tf_op jit(solution)/shard_map/ppermute | solution.py:383
  126.9 2.8 %collective-permute-done.30 = f32[3,64,128]{2,1,0:T(8,128)S(1)} collective-permute-done((f32[3,64,128]{2,1,0:T(8,128)S(1)}, f32[3,64,128]{2,1,0:T(8,128)S(1)}, u32[]{:S(2)}, u32[]{:S(2)}) %collective-permute-start.30) | collective-permute-done | bytes 98336 | tf_op jit(solution)/shard_map/ppermute | solution.py:383
  129.8 6.2 %collective-permute-start.31 = (f32[2,64,128]{2,1,0:T(8,128)S(1)}, f32[2,64,128]{2,1,0:T(8,128)S(1)}, u32[]{:S(2)}, u32[]{:S(2)}) collective-permute-start(f32[2,64,128]{2,1,0:T(8,128)S(1)} %fusion), channel_id=1, source_target_pairs={{0,1},{1,0},{2,3},{3,2},{4,5},{5,4},{6,7},{7,6},{8,9},{9,8},{10,11... | collective-permute-start | bytes 196616 | tf_op jit(solution)/shard_map/ppermute | solution.py:383
  (85 shorter events, 34.3 us)
Async XLA Ops:
  1.8 8.8 %collective-permute-start = (f32[2,64,256]{2,1,0:T(8,128)S(1)}, f32[2,64,256]{2,1,0:T(8,128)S(1)}, u32[]{:S(2)}, u32[]{:S(2)}) collective-permute-start(f32[2,64,256]{2,1,0:T(8,128)S(1)} %get-tuple-element.41), channel_id=1, source_target_pairs={{0,32},{1,33},{2,34},{3,35},{4,36},{5,37},{6,38},{7,39},{8,40},{9,... | collective-permute-start | bytes 393224 | tf_op jit(solution)/shard_map/ppermute | solution.py:375
  3.1 7.5 %collective-permute-start.1 = (f32[2,64,256]{2,1,0:T(8,128)S(1)}, f32[2,64,256]{2,1,0:T(8,128)S(1)}, u32[]{:S(2)}, u32[]{:S(2)}) collective-permute-start(f32[2,64,256]{2,1,0:T(8,128)S(1)} %get-tuple-element.42), channel_id=1, source_target_pairs={{0,224},{1,225},{2,226},{3,227},{4,228},{5,229},{6,230},{7,231},{8... | collective-permute-start | bytes 393224 | tf_op jit(solution)/shard_map/ppermute | solution.py:375
  5.5 14.8 %collective-permute-start.2 = (f32[2,128,128]{2,1,0:T(8,128)S(1)}, f32[2,128,128]{2,1,0:T(8,128)S(1)}, u32[]{:S(2)}, u32[]{:S(2)}) collective-permute-start(f32[2,128,128]{2,1,0:T(8,128)S(1)} %get-tuple-element.50), channel_id=1, source_target_pairs={{0,1},{1,2},{2,3},{3,4},{4,5},{5,6},{6,7},{7,8},{8,9},{9,10},{10,1... | collective-permute-start | bytes 393224 | tf_op jit(solution)/shard_map/ppermute | solution.py:375
  7.9 12.4 %collective-permute-start.3 = (f32[2,128,128]{2,1,0:T(8,128)S(1)}, f32[2,128,128]{2,1,0:T(8,128)S(1)}, u32[]{:S(2)}, u32[]{:S(2)}) collective-permute-start(f32[2,128,128]{2,1,0:T(8,128)S(1)} %get-tuple-element.51), channel_id=1, source_target_pairs={{0,31},{1,0},{2,1},{3,2},{4,3},{5,4},{6,5},{7,6},{8,7},{9,8},{10,9... | collective-permute-start | bytes 393224 | tf_op jit(solution)/shard_map/ppermute | solution.py:375
  11.3 9.0 %collective-permute-start.4 = (f32[2,64,128]{2,1,0:T(8,128)S(1)}, f32[2,64,128]{2,1,0:T(8,128)S(1)}, u32[]{:S(2)}, u32[]{:S(2)}) collective-permute-start(f32[2,64,128]{2,1,0:T(8,128)S(1)} %get-tuple-element.52), channel_id=1, source_target_pairs={{0,1},{1,2},{2,3},{3,4},{4,5},{5,6},{6,7},{7,8},{8,9},{9,10},{10,1... | collective-permute-start | bytes 196616 | tf_op jit(solution)/shard_map/ppermute | solution.py:375
  13.1 7.2 %collective-permute-start.5 = (f32[2,64,128]{2,1,0:T(8,128)S(1)}, f32[2,64,128]{2,1,0:T(8,128)S(1)}, u32[]{:S(2)}, u32[]{:S(2)}) collective-permute-start(f32[2,64,128]{2,1,0:T(8,128)S(1)} %get-tuple-element.53), channel_id=1, source_target_pairs={{0,31},{1,0},{2,1},{3,2},{4,3},{5,4},{6,5},{7,6},{8,7},{9,8},{10,9... | collective-permute-start | bytes 196616 | tf_op jit(solution)/shard_map/ppermute | solution.py:375
  30.5 17.4 %collective-permute-start.6 = (f32[2,384,128]{2,1,0:T(8,128)S(1)}, f32[2,384,128]{2,1,0:T(8,128)S(1)}, u32[]{:S(2)}, u32[]{:S(2)}) collective-permute-start(f32[2,384,128]{2,1,0:T(8,128)S(1)} %get-tuple-element.56), channel_id=1, source_target_pairs={{0,1},{1,2},{2,3},{3,4},{4,5},{5,6},{6,7},{7,8},{8,9},{9,10},{10,1... | collective-permute-start | bytes 1179656 | tf_op jit(solution)/shard_map/ppermute | solution.py:375
  30.5 17.4 %collective-permute-start.7 = (f32[2,384,128]{2,1,0:T(8,128)S(1)}, f32[2,384,128]{2,1,0:T(8,128)S(1)}, u32[]{:S(2)}, u32[]{:S(2)}) collective-permute-start(f32[2,384,128]{2,1,0:T(8,128)S(1)} %get-tuple-element.57), channel_id=1, source_target_pairs={{0,31},{1,0},{2,1},{3,2},{4,3},{5,4},{6,5},{7,6},{8,7},{9,8},{10,9... | collective-permute-start | bytes 1179656 | tf_op jit(solution)/shard_map/ppermute | solution.py:375
  31.5 6.0 %collective-permute-start.11 = (f32[3,64,128]{2,1,0:T(8,128)S(1)}, f32[3,64,128]{2,1,0:T(8,128)S(1)}, u32[]{:S(2)}, u32[]{:S(2)}) collective-permute-start(f32[3,64,128]{2,1,0:T(8,128)S(1)} %add.94), channel_id=1, source_target_pairs={{0,32},{1,129},{2,34},{3,131},{4,36},{5,133},{6,38},{7,135},{8,40}... | collective-permute-start | bytes 294920 | tf_op jit(solution)/shard_map/ppermute | solution.py:383
  42.3 7.7 %collective-permute-start.13 = (f32[3,64,128]{2,1,0:T(8,128)S(1)}, f32[3,64,128]{2,1,0:T(8,128)S(1)}, u32[]{:S(2)}, u32[]{:S(2)}) collective-permute-start(f32[3,64,128]{2,1,0:T(8,128)S(1)} %add.96), channel_id=1, source_target_pairs={{0,2},{1,153},{2,0},{3,155},{4,6},{5,157},{6,4},{7,159},{8,10},{9,... | collective-permute-start | bytes 294920 | tf_op jit(solution)/shard_map/ppermute | solution.py:383
  50.1 20.2 %collective-permute-start.8 = (f32[2,3,128,128]{3,2,1,0:T(8,128)S(1)}, f32[2,3,128,128]{3,2,1,0:T(8,128)S(1)}, u32[]{:S(2)}, u32[]{:S(2)}) collective-permute-start(f32[2,3,128,128]{3,2,1,0:T(8,128)S(1)} %get-tuple-element.59), channel_id=1, source_target_pairs={{0,32},{1,33},{2,34},{3,35},{4,36},{5,37},{6,38},{7,39},{8,40},{9,... | collective-permute-start | bytes 1179656 | tf_op jit(solution)/shard_map/ppermute | solution.py:375
  51.1 19.2 %collective-permute-start.9 = (f32[2,3,128,128]{3,2,1,0:T(8,128)S(1)}, f32[2,3,128,128]{3,2,1,0:T(8,128)S(1)}, u32[]{:S(2)}, u32[]{:S(2)}) collective-permute-start(f32[2,3,128,128]{3,2,1,0:T(8,128)S(1)} %get-tuple-element.60), channel_id=1, source_target_pairs={{0,224},{1,225},{2,226},{3,227},{4,228},{5,229},{6,230},{7,231},{8... | collective-permute-start | bytes 1179656 | tf_op jit(solution)/shard_map/ppermute | solution.py:375
  54.8 8.3 %collective-permute-start.15 = (f32[3,64,128]{2,1,0:T(8,128)S(1)}, f32[3,64,128]{2,1,0:T(8,128)S(1)}, u32[]{:S(2)}, u32[]{:S(2)}) collective-permute-start(f32[3,64,128]{2,1,0:T(8,128)S(1)} %add.100), channel_id=1, source_target_pairs={{0,128},{1,7},{2,130},{3,5},{4,132},{5,3},{6,134},{7,1},{8,136},{9... | collective-permute-start | bytes 294920 | tf_op jit(solution)/shard_map/ppermute | solution.py:383
  67.0 5.3 %collective-permute-start.17 = (f32[3,64,128]{2,1,0:T(8,128)S(1)}, f32[3,64,128]{2,1,0:T(8,128)S(1)}, u32[]{:S(2)}, u32[]{:S(2)}) collective-permute-start(f32[3,64,128]{2,1,0:T(8,128)S(1)} %add.102), channel_id=1, source_target_pairs={{0,152},{1,97},{2,154},{3,99},{4,156},{5,101},{6,158},{7,103},{8,1... | collective-permute-start | bytes 294920 | tf_op jit(solution)/shard_map/ppermute | solution.py:383
  72.3 12.4 %collective-permute-start.18 = (f32[2,64,128]{2,1,0:T(8,128)S(1)}, f32[2,64,128]{2,1,0:T(8,128)S(1)}, u32[]{:S(2)}, u32[]{:S(2)}) collective-permute-start(f32[2,64,128]{2,1,0:T(8,128)S(1)} %fusion.1.refs_10_), channel_id=1, source_target_pairs={{0,1},{1,0},{2,3},{3,2},{4,5},{5,4},{6,7},{7,6},{8,9},{9,8},{10,11... | collective-permute-start | bytes 196616 | tf_op jit(solution)/shard_map/ppermute | solution.py:383
  93.5 12.0 %collective-permute-start.19 = (f32[2,192,128]{2,1,0:T(8,128)S(1)}, f32[2,192,128]{2,1,0:T(8,128)S(1)}, u32[]{:S(2)}, u32[]{:S(2)}) collective-permute-start(f32[2,192,128]{2,1,0:T(8,128)S(1)} %get-tuple-element.69), channel_id=1, source_target_pairs={{0,1},{1,2},{2,3},{3,4},{4,5},{5,6},{6,7},{7,8},{8,9},{9,10},{10,1... | collective-permute-start | bytes 589832 | tf_op jit(solution)/shard_map/ppermute | solution.py:375
  93.6 11.9 %collective-permute-start.20 = (f32[2,192,128]{2,1,0:T(8,128)S(1)}, f32[2,192,128]{2,1,0:T(8,128)S(1)}, u32[]{:S(2)}, u32[]{:S(2)}) collective-permute-start(f32[2,192,128]{2,1,0:T(8,128)S(1)} %get-tuple-element.70), channel_id=1, source_target_pairs={{0,31},{1,0},{2,1},{3,2},{4,3},{5,4},{6,5},{7,6},{8,7},{9,8},{10,9... | collective-permute-start | bytes 589832 | tf_op jit(solution)/shard_map/ppermute | solution.py:375
  97.3 5.0 %collective-permute-start.25 = (f32[3,64,128]{2,1,0:T(8,128)S(1)}, f32[3,64,128]{2,1,0:T(8,128)S(1)}, u32[]{:S(2)}, u32[]{:S(2)}) collective-permute-start(f32[3,64,128]{2,1,0:T(8,128)S(1)} %add.108), channel_id=1, source_target_pairs={{0,96},{1,9},{2,98},{3,11},{4,100},{5,13},{6,102},{7,15},{8,104},{... | collective-permute-start | bytes 294920 | tf_op jit(solution)/shard_map/ppermute | solution.py:383
  102.3 6.7 %collective-permute-start.26 = (f32[3,64,128]{2,1,0:T(8,128)S(1)}, f32[3,64,128]{2,1,0:T(8,128)S(1)}, u32[]{:S(2)}, u32[]{:S(2)}) collective-permute-start(f32[3,64,128]{2,1,0:T(8,128)S(1)} %add.109), channel_id=1, source_target_pairs={{0,2},{1,153},{2,0},{3,155},{4,6},{5,157},{6,4},{7,159},{8,10},{9,... | collective-permute-start | bytes 294920 | tf_op jit(solution)/shard_map/ppermute | solution.py:383
  112.5 6.8 %collective-permute-start.28 = (f32[3,64,128]{2,1,0:T(8,128)S(1)}, f32[3,64,128]{2,1,0:T(8,128)S(1)}, u32[]{:S(2)}, u32[]{:S(2)}) collective-permute-start(f32[3,64,128]{2,1,0:T(8,128)S(1)} %add.113), channel_id=1, source_target_pairs={{0,128},{1,7},{2,130},{3,5},{4,132},{5,3},{6,134},{7,1},{8,136},{9... | collective-permute-start | bytes 294920 | tf_op jit(solution)/shard_map/ppermute | solution.py:383
  115.7 9.4 %collective-permute-start.21 = (f32[2,3,64,128]{3,2,1,0:T(8,128)S(1)}, f32[2,3,64,128]{3,2,1,0:T(8,128)S(1)}, u32[]{:S(2)}, u32[]{:S(2)}) collective-permute-start(f32[2,3,64,128]{3,2,1,0:T(8,128)S(1)} %get-tuple-element.72), channel_id=1, source_target_pairs={{0,32},{1,33},{2,34},{3,35},{4,36},{5,37},{6,38},{7,39},{8,40},{9,... | collective-permute-start | bytes 589832 | tf_op jit(solution)/shard_map/ppermute | solution.py:375
  117.3 7.8 %collective-permute-start.22 = (f32[2,3,64,128]{3,2,1,0:T(8,128)S(1)}, f32[2,3,64,128]{3,2,1,0:T(8,128)S(1)}, u32[]{:S(2)}, u32[]{:S(2)}) collective-permute-start(f32[2,3,64,128]{3,2,1,0:T(8,128)S(1)} %get-tuple-element.73), channel_id=1, source_target_pairs={{0,224},{1,225},{2,226},{3,227},{4,228},{5,229},{6,230},{7,231},{8... | collective-permute-start | bytes 589832 | tf_op jit(solution)/shard_map/ppermute | solution.py:375
  119.3 5.6 %collective-permute-start.29 = (f32[3,64,128]{2,1,0:T(8,128)S(1)}, f32[3,64,128]{2,1,0:T(8,128)S(1)}, u32[]{:S(2)}, u32[]{:S(2)}) collective-permute-start(f32[3,64,128]{2,1,0:T(8,128)S(1)} %add.114), channel_id=1, source_target_pairs={{0,8},{1,33},{2,10},{3,35},{4,12},{5,37},{6,14},{7,39},{8,0},{9,41... | collective-permute-start | bytes 294920 | tf_op jit(solution)/shard_map/ppermute | solution.py:383
  129.8 7.1 %collective-permute-start.31 = (f32[2,64,128]{2,1,0:T(8,128)S(1)}, f32[2,64,128]{2,1,0:T(8,128)S(1)}, u32[]{:S(2)}, u32[]{:S(2)}) collective-permute-start(f32[2,64,128]{2,1,0:T(8,128)S(1)} %fusion), channel_id=1, source_target_pairs={{0,1},{1,0},{2,3},{3,2},{4,5},{5,4},{6,7},{7,6},{8,9},{9,8},{10,11... | collective-permute-start | bytes 196616 | tf_op jit(solution)/shard_map/ppermute | solution.py:383
  (13 other events, 53.1 us)

commit v3 on v2

--- a/solution.py
+++ b/solution.py
@@ -13,7 +13,7 @@
 TILE = 256
 EXT = TILE + WIDTH
 BLOCKS = EXT // WIDTH
-GROUP = 4
+GROUP = 8
 CHAINS = 2
 VMEM_LIMIT = 16 * 1024 * 1024
 
@@ -75,17 +75,11 @@
 def plan_kernel(flags_ref, slots_ref):
     iterations, cap = flags_ref.shape
     for step in range(iterations):
-
-        def note(slot, count):
-            live = flags_ref[step, slot] != 0
-
-            @pl.when(live)
-            def _():
-                slots_ref[step, count] = slot
-
-            return count + live.astype(jnp.int32)
-
-        slots_ref[step, cap] = lax.fori_loop(0, cap, note, jnp.int32(0))
+        count = jnp.int32(0)
+        for slot in range(cap):
+            slots_ref[step, count] = slot
+            count = count + flags_ref[step, slot]
+        slots_ref[step, cap] = count
 
 
 def prepare_kernel(after_ref, amp_ref, probe_ref, ra_ref, lb_ref, la_ref, rb_ref, amp_out, probe_out):
@@ -164,9 +158,10 @@
             ext_ref[part, 2, rows, :] = jnp.where(low, second, gate(right, has[3]))
 
 
-def patterns_kernel(first, last, *refs):
-    (slots_ref, rows_ref, cols_ref, where_ref), refs = refs[:4], refs[4:]
-    cap = rows_ref.shape[0]
+def patterns_kernel(step, last, *refs):
+    (slots_ref, centres_ref, where_ref), refs = refs[:3], refs[3:]
+    first = step == 0
+    cap = centres_ref.shape[1]
     if first:
         (amp_ref, ra_ref, lb_ref, la_ref, rb_ref), halo, refs = refs[:5], refs[5:12], refs[12:]
         probe_ref, refs = refs[0], refs[1:]
@@ -180,15 +175,15 @@
         there = pl.multiple_of((1 - where_ref[4]) * RIM, RIM)
         probe_ref[:, pl.ds(here, RIM), :] = held_mine[...]
         probe_ref[:, pl.ds(there, RIM), :] = held_other[...]
-    count = slots_ref[cap]
+    count = slots_ref[step, cap]
     acc_ref[...] = jnp.zeros_like(acc_ref)
     sums_ref[...] = jnp.zeros_like(sums_ref)
     lane = lane_of(WIDTH)
 
     def where_is(slot):
-        left = cols_ref[slot]
+        left = centres_ref[1, slot]
         block = left // WIDTH
-        return rows_ref[slot], block, left - block * WIDTH
+        return centres_ref[0, slot], block, left - block * WIDTH
 
     def patch(slot):
         top, block, shift = where_is(slot)
@@ -208,7 +203,7 @@
             acc_ref[part, block + 1, pl.ds(top, WIDTH), :] += jnp.where(lane < shift, rolled, 0.0)
 
     def several(base):
-        chosen = [slots_ref[jnp.minimum(base + i, count - 1)] for i in range(GROUP)]
+        chosen = [slots_ref[step, jnp.minimum(base + i, count - 1)] for i in range(GROUP)]
         keep = [(base + i < count).astype(jnp.float32) for i in range(GROUP)]
         pr, pi = probe_ref[0], probe_ref[1]
         waves = []
@@ -382,14 +377,18 @@
         ]
         return lax.ppermute(value, ("row", "col"), pairs)
 
-    x_steps = ((1, 0), (3, 0))
-    y_steps = ((0, 2), (0, 6))
-    z_steps = ((4, 0), (0, 8), (4, 24))
-    ladder = tuple(zip(x_steps + y_steps + z_steps, z_steps + y_steps + x_steps))
+    x_steps = ((1, 0), (2, 0), (3, 0))
+    y_steps = ((0, 2), (0, 4), (0, 6))
+    z_steps = ((4, 0), (0, 8), (4, 8))
+    z_far = (4, 24)
+
+    def four(value, steps):
+        one, two, three = (swap(value, *bits) for bits in steps)
+        return (value + one) + (two + three)
+
     twin = ((0, 1), (0, 1))
     iterations, cap = members.shape[0], members.shape[3]
-    rows = centres[0, 0, 0]
-    cols = centres[1, 0, 0]
+    places = centres[:, 0, 0]
     row, col = lax.axis_index("row"), lax.axis_index("col")
     where = jnp.stack(
         [row > 0, row < rows_n - 1, col > 0, col < cols_n - 1, col % 2 == 1]
@@ -427,8 +426,8 @@
         size = RIM if last else WIDTH
         strip = (2, EXT // 2, WIDTH) if last else (2, EXT, WIDTH)
         outs = (ext_shape, strip, strip) + ((3, RIM, WIDTH),) * 2 + (corner,)
-        kernel = functools.partial(patterns_kernel, first, last)
-        scalars = (slots[step], rows, cols, where)
+        kernel = functools.partial(patterns_kernel, step, last)
+        scalars = (slots, places, where)
         if first:
             acc, east, west, mine, other, held, ext = local_call(
                 kernel, "patterns", scalars, (*kept, *halo, probe), outs + (ext_shape,), sums_scratch
@@ -441,23 +440,20 @@
         from_left = shift(east, 0, 1)
         from_right = shift(west, 0, -1)
         total = mine + swap(other, *twin)
-        total = total + swap(total, *ladder[0])
-        total = total + swap(total, *ladder[1])
+        total = four(total, tuple(zip(x_steps, y_steps)))
         acc, to_down, to_up, token = local_call(
             functools.partial(fold_kernel, last), "fold", (where,), (acc, from_left, from_right),
             (ext_shape,) + ((2, BLOCKS, size, WIDTH),) * 2 + ((RIM, WIDTH),),
         )
         up = shift(to_down, 1, 0)
         down = shift(to_up, -1, 0)
-        total = total + swap(total, *ladder[2]) + token
-        total = total + swap(total, *ladder[3])
-        total = total + swap(total, *ladder[4])
-        total = total + swap(total, *ladder[5])
+        total = four(total, tuple(zip(y_steps, x_steps))) + token
+        total = four(total, tuple(zip(z_steps, z_steps)))
         ext, token = local_call(
             finish_kernel if last else update_kernel, "finish" if last else "update", (where,),
             (probe, ext, acc, up, down), (obj.shape if last else ext_shape, (RIM, WIDTH)),
         )
-        total = total + swap(total, *ladder[6]) + token
+        total = total + swap(total, z_far, z_far) + token
         held = held - total[:2] / (total[2] + 1e-06)
         halves = (held, swap(held, *twin))
     held, other = halves

time: 138 us -> 123 us (0.89)
  the two profiles are of different devices: /device:TPU:33 before, /device:TPU:25 now
where the time goes in v3:
time: 123 us; the launch traced here: 122 us
  starting transfers between devices  56.9 us (46%)
  waiting for transfers between devices  40.3 us (33%)
  Pallas kernels  19.5 us (16%)
  local copies, waits for them, and re-layouts  3.95 us (3%)
    ppermute x24, starting transfers between devices, swap(): return lax.ppermute(value, ('row', 'col'), pairs)  31.6 us
    ppermute x14, waiting for transfers between devices, shift(): return lax.ppermute(value, ('row', 'col'), pairs)  28.2 us
    ppermute x14, starting transfers between devices, shift(): return lax.ppermute(value, ('row', 'col'), pairs)  25.3 us
    pallas_call x10, Pallas kernels, local_call(): pl.pallas_call(kernel, out_shape=shapes, in_specs=[smem] * len(scalars) +...  19.5 us
    ppermute x24, waiting for transfers between devices, swap(): return lax.ppermute(value, ('row', 'col'), pairs)  12 us
    unnamed x12, local copies, waits for them, and re-layouts  3.84 us
  transfers between devices with their start and end apart: 38, of which 16 were waited for; matrix products, arithmetic and copies ran while one was open for 0% of the time, Pallas kernels for 5%

profile of v3, /device:TPU:25, one launch (start us, length us, event | category | flops | bytes accessed | tf_op | source)
XLA Modules:
  0.0 122.5 jit_solution(14475235446736555783)
XLA Ops:
  3.1 2.7 %collective-permute-start.1 = (f32[2,64,256]{2,1,0:T(8,128)S(1)}, f32[2,64,256]{2,1,0:T(8,128)S(1)}, u32[]{:S(2)}, u32[]{:S(2)}) collective-permute-start(f32[2,64,256]{2,1,0:T(8,128)S(1)} %get-tuple-element.42), channel_id=1, source_target_pairs={{0,224},{1,225},{2,226},{3,227},{4,228},{5,229},{6,230},{7,231},{8... | collective-permute-start | bytes 393224 | tf_op jit(solution)/shard_map/ppermute | solution.py:370
  5.8 3.5 %collective-permute-start.2 = (f32[2,128,128]{2,1,0:T(8,128)S(1)}, f32[2,128,128]{2,1,0:T(8,128)S(1)}, u32[]{:S(2)}, u32[]{:S(2)}) collective-permute-start(f32[2,128,128]{2,1,0:T(8,128)S(1)} %get-tuple-element.50), channel_id=1, source_target_pairs={{0,1},{1,2},{2,3},{3,4},{4,5},{5,6},{6,7},{7,8},{8,9},{9,10},{10,1... | collective-permute-start | bytes 393224 | tf_op jit(solution)/shard_map/ppermute | solution.py:370
  10.1 4.8 %collective-permute-start.4 = (f32[2,64,128]{2,1,0:T(8,128)S(1)}, f32[2,64,128]{2,1,0:T(8,128)S(1)}, u32[]{:S(2)}, u32[]{:S(2)}) collective-permute-start(f32[2,64,128]{2,1,0:T(8,128)S(1)} %get-tuple-element.52), channel_id=1, source_target_pairs={{0,1},{1,2},{2,3},{3,4},{4,5},{5,6},{6,7},{7,8},{8,9},{9,10},{10,1... | collective-permute-start | bytes 196616 | tf_op jit(solution)/shard_map/ppermute | solution.py:370
  19.5 2.1 %collective-permute-done.5.refs_14_ = f32[2,64,128]{2,1,0:T(8,128)S(1)} collective-permute-done((f32[2,64,128]{2,1,0:T(8,128)S(1)}, f32[2,64,128]{2,1,0:T(8,128)S(1)}, u32[]{:S(2)}, u32[]{:S(2)}) %collective-permute-start.5) | collective-permute-done | bytes 65568 | tf_op jit(solution)/shard_map/ppermute | solution.py:370
  21.6 6.4 %patterns.2 = (f32[2,3,384,128]{3,2,1,0:T(8,128)S(1)}, f32[2,384,128]{2,1,0:T(8,128)S(1)}, f32[2,384,128]{2,1,0:T(8,128)S(1)}, f32[3,64,128]{2,1,0:T(8,128)S(1)}...) custom-call(s32[2,33]{1,0:T(2,128)S(1)} %plan.1.refs_0_, ...), custom_call_target="tpu_custom_call" | custom-call | tf_op jit(solution)/shard_map/patterns/pallas_call | solution.py:352
  29.5 4.2 %collective-permute-start.13 = (f32[3,64,128]{2,1,0:T(8,128)S(1)}, f32[3,64,128]{2,1,0:T(8,128)S(1)}, u32[]{:S(2)}, u32[]{:S(2)}) collective-permute-start(f32[3,64,128]{2,1,0:T(8,128)S(1)} %add.112), channel_id=1, source_target_pairs={{0,96},{1,7},{2,98},{3,5},{4,100},{5,3},{6,102},{7,1},{8,104},{9,1... | collective-permute-start | bytes 294920 | tf_op jit(solution)/shard_map/ppermute | solution.py:378
  34.0 1.8 %collective-permute-start.6 = (f32[2,384,128]{2,1,0:T(8,128)S(1)}, f32[2,384,128]{2,1,0:T(8,128)S(1)}, u32[]{:S(2)}, u32[]{:S(2)}) collective-permute-start(f32[2,384,128]{2,1,0:T(8,128)S(1)} %get-tuple-element.56), channel_id=1, source_target_pairs={{0,1},{1,2},{2,3},{3,4},{4,5},{5,6},{6,7},{7,8},{8,9},{9,10},{10,1... | collective-permute-start | bytes 1179656 | tf_op jit(solution)/shard_map/ppermute | solution.py:370
  41.6 8.6 %collective-permute-done.7.from_right = f32[2,384,128]{2,1,0:T(8,128)S(1)} collective-permute-done((f32[2,384,128]{2,1,0:T(8,128)S(1)}, f32[2,384,128]{2,1,0:T(8,128)S(1)}, u32[]{:S(2)}, u32[]{:S(2)}) %collective-permute-start.7) | collective-permute-done | bytes 393248 | tf_op jit(solution)/shard_map/ppermute | solution.py:370
  51.1 6.5 %collective-permute-start.18 = (f32[3,64,128]{2,1,0:T(8,128)S(1)}, f32[3,64,128]{2,1,0:T(8,128)S(1)}, u32[]{:S(2)}, u32[]{:S(2)}) collective-permute-start(f32[3,64,128]{2,1,0:T(8,128)S(1)} %add_add_fusion.6), channel_id=1, source_target_pairs={{0,8},{1,9},{2,10},{3,11},{4,12},{5,13},{6,14},{7,15},{8,0},{9,1},... | collective-permute-start | bytes 294920 | tf_op jit(solution)/shard_map/ppermute | solution.py:378
  57.6 4.3 %collective-permute-start.19 = (f32[3,64,128]{2,1,0:T(8,128)S(1)}, f32[3,64,128]{2,1,0:T(8,128)S(1)}, u32[]{:S(2)}, u32[]{:S(2)}) collective-permute-start(f32[3,64,128]{2,1,0:T(8,128)S(1)} %add_add_fusion.6), channel_id=1, source_target_pairs={{0,136},{1,137},{2,138},{3,139},{4,140},{5,141},{6,142},{7,143},{8... | collective-permute-start | bytes 294920 | tf_op jit(solution)/shard_map/ppermute | solution.py:378
  62.1 3.6 %collective-permute-start.9 = (f32[2,3,128,128]{3,2,1,0:T(8,128)S(1)}, f32[2,3,128,128]{3,2,1,0:T(8,128)S(1)}, u32[]{:S(2)}, u32[]{:S(2)}) collective-permute-start(f32[2,3,128,128]{3,2,1,0:T(8,128)S(1)} %get-tuple-element.60), channel_id=1, source_target_pairs={{0,224},{1,225},{2,226},{3,227},{4,228},{5,229},{6,230},{7,231},{8... | collective-permute-start | bytes 1179656 | tf_op jit(solution)/shard_map/ppermute | solution.py:370
  67.4 5.6 %collective-permute-done.8.up = f32[2,3,128,128]{3,2,1,0:T(8,128)S(1)} collective-permute-done((f32[2,3,128,128]{3,2,1,0:T(8,128)S(1)}, f32[2,3,128,128]{3,2,1,0:T(8,128)S(1)}, u32[]{:S(2)}, u32[]{:S(2)}) %collective-permute-start.8) | collective-permute-done | bytes 393248 | tf_op jit(solution)/shard_map/ppermute | solution.py:370
  75.3 6.5 %patterns.3 = (f32[2,3,384,128]{3,2,1,0:T(8,128)S(1)}, f32[2,192,128]{2,1,0:T(8,128)S(1)}, f32[2,192,128]{2,1,0:T(8,128)S(1)}, f32[3,64,128]{2,1,0:T(8,128)S(1)}...) custom-call(s32[2,33]{1,0:T(2,128)S(1)} %plan.1.refs_0_, s32[2,32]{1,0:T(2,128)S(1)} %bitcast.14, ...), custom_call_target="tpu_custom_call" | custom-call | tf_op jit(solution)/shard_map/patterns/pallas_call | solution.py:352
  83.4 2.5 %collective-permute-start.27 = (f32[3,64,128]{2,1,0:T(8,128)S(1)}, f32[3,64,128]{2,1,0:T(8,128)S(1)}, u32[]{:S(2)}, u32[]{:S(2)}) collective-permute-start(f32[3,64,128]{2,1,0:T(8,128)S(1)} %add.128), channel_id=1, source_target_pairs={{0,32},{1,3},{2,34},{3,1},{4,36},{5,7},{6,38},{7,5},{8,40},{9,11},... | collective-permute-start | bytes 294920 | tf_op jit(solution)/shard_map/ppermute | solution.py:378
  85.9 4.0 %collective-permute-start.22 = (f32[2,192,128]{2,1,0:T(8,128)S(1)}, f32[2,192,128]{2,1,0:T(8,128)S(1)}, u32[]{:S(2)}, u32[]{:S(2)}) collective-permute-start(f32[2,192,128]{2,1,0:T(8,128)S(1)} %get-tuple-element.69), channel_id=1, source_target_pairs={{0,1},{1,2},{2,3},{3,4},{4,5},{5,6},{6,7},{7,8},{8,9},{9,10},{10,1... | collective-permute-start | bytes 589832 | tf_op jit(solution)/shard_map/ppermute | solution.py:370
  92.8 1.9 %collective-permute-done.22.from_left = f32[2,192,128]{2,1,0:T(8,128)S(1)} collective-permute-done((f32[2,192,128]{2,1,0:T(8,128)S(1)}, f32[2,192,128]{2,1,0:T(8,128)S(1)}, u32[]{:S(2)}, u32[]{:S(2)}) %collective-permute-start.22) | collective-permute-done | bytes 196640 | tf_op jit(solution)/shard_map/ppermute | solution.py:370
  94.7 3.6 %collective-permute-done.23.from_right = f32[2,192,128]{2,1,0:T(8,128)S(1)} collective-permute-done((f32[2,192,128]{2,1,0:T(8,128)S(1)}, f32[2,192,128]{2,1,0:T(8,128)S(1)}, u32[]{:S(2)}, u32[]{:S(2)}) %collective-permute-start.23) | collective-permute-done | bytes 196640 | tf_op jit(solution)/shard_map/ppermute | solution.py:370
  99.0 3.6 %collective-permute-start.34 = (f32[3,64,128]{2,1,0:T(8,128)S(1)}, f32[3,64,128]{2,1,0:T(8,128)S(1)}, u32[]{:S(2)}, u32[]{:S(2)}) collective-permute-start(f32[3,64,128]{2,1,0:T(8,128)S(1)} %add_add_fusion.2), channel_id=1, source_target_pairs={{0,8},{1,9},{2,10},{3,11},{4,12},{5,13},{6,14},{7,15},{8,0},{9,1},... | collective-permute-start | bytes 294920 | tf_op jit(solution)/shard_map/ppermute | solution.py:378
  103.9 2.6 %collective-permute-start.25 = (f32[2,3,64,128]{3,2,1,0:T(8,128)S(1)}, f32[2,3,64,128]{3,2,1,0:T(8,128)S(1)}, u32[]{:S(2)}, u32[]{:S(2)}) collective-permute-start(f32[2,3,64,128]{3,2,1,0:T(8,128)S(1)} %get-tuple-element.73), channel_id=1, source_target_pairs={{0,224},{1,225},{2,226},{3,227},{4,228},{5,229},{6,230},{7,231},{8... | collective-permute-start | bytes 589832 | tf_op jit(solution)/shard_map/ppermute | solution.py:370
  106.6 3.6 %collective-permute-done.34 = f32[3,64,128]{2,1,0:T(8,128)S(1)} collective-permute-done((f32[3,64,128]{2,1,0:T(8,128)S(1)}, f32[3,64,128]{2,1,0:T(8,128)S(1)}, u32[]{:S(2)}, u32[]{:S(2)}) %collective-permute-start.34) | collective-permute-done | bytes 98336 | tf_op jit(solution)/shard_map/ppermute | solution.py:378
  110.8 1.6 %collective-permute-start.36 = (f32[3,64,128]{2,1,0:T(8,128)S(1)}, f32[3,64,128]{2,1,0:T(8,128)S(1)}, u32[]{:S(2)}, u32[]{:S(2)}) collective-permute-start(f32[3,64,128]{2,1,0:T(8,128)S(1)} %add_add_fusion.1), channel_id=1, source_target_pairs={{0,152},{1,153},{2,154},{3,155},{4,156},{5,157},{6,158},{7,159},{8... | collective-permute-start | bytes 294920 | tf_op jit(solution)/shard_map/ppermute | solution.py:378
  112.4 4.9 %collective-permute-done.24.up = f32[2,3,64,128]{3,2,1,0:T(8,128)S(1)} collective-permute-done((f32[2,3,64,128]{3,2,1,0:T(8,128)S(1)}, f32[2,3,64,128]{3,2,1,0:T(8,128)S(1)}, u32[]{:S(2)}, u32[]{:S(2)}) %collective-permute-start.24) | collective-permute-done | bytes 196640 | tf_op jit(solution)/shard_map/ppermute | solution.py:370
  117.3 1.8 %finish.1 = (f32[2,256,256]{2,1,0:T(8,128)}, f32[64,128]{1,0:T(8,128)S(1)}) custom-call(s32[5]{0:T(128)S(1)} %convert_element_type.3.where_ref.refs_2_, f32[2,128,128]{2,1,0:T(8,128)S(1)} %get-tuple-element.67.probe_ref, f32[2,3,384,128]{3,2,1,0:T(8,128)S(1)} %get-tuple-element.61.refs_8_.ext_ref, f32[2,3,384,128]{3,2,1,0:T(8,128)S(1)} %get-tuple-element.71.acc_ref, ...), custom_call_target="tpu_custom_call" | custom-call | tf_op jit(solution)/shard_map/finish/pallas_call | solution.py:352
  119.1 1.8 %collective-permute-start.37 = (f32[2,64,128]{2,1,0:T(8,128)S(1)}, f32[2,64,128]{2,1,0:T(8,128)S(1)}, u32[]{:S(2)}, u32[]{:S(2)}) collective-permute-start(f32[2,64,128]{2,1,0:T(8,128)S(1)} %fusion), channel_id=1, source_target_pairs={{0,1},{1,0},{2,3},{3,2},{4,5},{5,4},{6,7},{7,6},{8,9},{9,8},{10,11... | collective-permute-start | bytes 196616 | tf_op jit(solution)/shard_map/ppermute | solution.py:378
  (91 shorter events, 29.1 us)
Async XLA Ops:
  1.8 7.6 %collective-permute-start = (f32[2,64,256]{2,1,0:T(8,128)S(1)}, f32[2,64,256]{2,1,0:T(8,128)S(1)}, u32[]{:S(2)}, u32[]{:S(2)}) collective-permute-start(f32[2,64,256]{2,1,0:T(8,128)S(1)} %get-tuple-element.41), channel_id=1, source_target_pairs={{0,32},{1,33},{2,34},{3,35},{4,36},{5,37},{6,38},{7,39},{8,40},{9,... | collective-permute-start | bytes 393224 | tf_op jit(solution)/shard_map/ppermute | solution.py:370
  5.8 13.7 %collective-permute-start.2 = (f32[2,128,128]{2,1,0:T(8,128)S(1)}, f32[2,128,128]{2,1,0:T(8,128)S(1)}, u32[]{:S(2)}, u32[]{:S(2)}) collective-permute-start(f32[2,128,128]{2,1,0:T(8,128)S(1)} %get-tuple-element.50), channel_id=1, source_target_pairs={{0,1},{1,2},{2,3},{3,4},{4,5},{5,6},{6,7},{7,8},{8,9},{9,10},{10,1... | collective-permute-start | bytes 393224 | tf_op jit(solution)/shard_map/ppermute | solution.py:370
  9.3 10.2 %collective-permute-start.3 = (f32[2,128,128]{2,1,0:T(8,128)S(1)}, f32[2,128,128]{2,1,0:T(8,128)S(1)}, u32[]{:S(2)}, u32[]{:S(2)}) collective-permute-start(f32[2,128,128]{2,1,0:T(8,128)S(1)} %get-tuple-element.51), channel_id=1, source_target_pairs={{0,31},{1,0},{2,1},{3,2},{4,3},{5,4},{6,5},{7,6},{8,7},{9,8},{10,9... | collective-permute-start | bytes 393224 | tf_op jit(solution)/shard_map/ppermute | solution.py:370
  10.1 9.4 %collective-permute-start.4 = (f32[2,64,128]{2,1,0:T(8,128)S(1)}, f32[2,64,128]{2,1,0:T(8,128)S(1)}, u32[]{:S(2)}, u32[]{:S(2)}) collective-permute-start(f32[2,64,128]{2,1,0:T(8,128)S(1)} %get-tuple-element.52), channel_id=1, source_target_pairs={{0,1},{1,2},{2,3},{3,4},{4,5},{5,6},{6,7},{7,8},{8,9},{9,10},{10,1... | collective-permute-start | bytes 196616 | tf_op jit(solution)/shard_map/ppermute | solution.py:370
  34.0 7.7 %collective-permute-start.6 = (f32[2,384,128]{2,1,0:T(8,128)S(1)}, f32[2,384,128]{2,1,0:T(8,128)S(1)}, u32[]{:S(2)}, u32[]{:S(2)}) collective-permute-start(f32[2,384,128]{2,1,0:T(8,128)S(1)} %get-tuple-element.56), channel_id=1, source_target_pairs={{0,1},{1,2},{2,3},{3,4},{4,5},{5,6},{6,7},{7,8},{8,9},{9,10},{10,1... | collective-permute-start | bytes 1179656 | tf_op jit(solution)/shard_map/ppermute | solution.py:370
  35.7 14.5 %collective-permute-start.7 = (f32[2,384,128]{2,1,0:T(8,128)S(1)}, f32[2,384,128]{2,1,0:T(8,128)S(1)}, u32[]{:S(2)}, u32[]{:S(2)}) collective-permute-start(f32[2,384,128]{2,1,0:T(8,128)S(1)} %get-tuple-element.57), channel_id=1, source_target_pairs={{0,31},{1,0},{2,1},{3,2},{4,3},{5,4},{6,5},{7,6},{8,7},{9,8},{10,9... | collective-permute-start | bytes 1179656 | tf_op jit(solution)/shard_map/ppermute | solution.py:370
  37.3 13.7 %collective-permute-start.15 = (f32[3,64,128]{2,1,0:T(8,128)S(1)}, f32[3,64,128]{2,1,0:T(8,128)S(1)}, u32[]{:S(2)}, u32[]{:S(2)}) collective-permute-start(f32[3,64,128]{2,1,0:T(8,128)S(1)} %add_add_fusion.7), channel_id=1, source_target_pairs={{0,4},{1,65},{2,6},{3,67},{4,0},{5,69},{6,2},{7,71},{8,12},{9,73},... | collective-permute-start | bytes 294920 | tf_op jit(solution)/shard_map/ppermute | solution.py:378
  37.8 13.2 %collective-permute-start.16 = (f32[3,64,128]{2,1,0:T(8,128)S(1)}, f32[3,64,128]{2,1,0:T(8,128)S(1)}, u32[]{:S(2)}, u32[]{:S(2)}) collective-permute-start(f32[3,64,128]{2,1,0:T(8,128)S(1)} %add_add_fusion.7), channel_id=1, source_target_pairs={{0,6},{1,97},{2,4},{3,99},{4,2},{5,101},{6,0},{7,103},{8,14},{9,10... | collective-permute-start | bytes 294920 | tf_op jit(solution)/shard_map/ppermute | solution.py:378
  39.3 11.7 %collective-permute-start.14 = (f32[3,64,128]{2,1,0:T(8,128)S(1)}, f32[3,64,128]{2,1,0:T(8,128)S(1)}, u32[]{:S(2)}, u32[]{:S(2)}) collective-permute-start(f32[3,64,128]{2,1,0:T(8,128)S(1)} %add_add_fusion.7), channel_id=1, source_target_pairs={{0,2},{1,33},{2,0},{3,35},{4,6},{5,37},{6,4},{7,39},{8,10},{9,41},... | collective-permute-start | bytes 294920 | tf_op jit(solution)/shard_map/ppermute | solution.py:378
  51.1 14.6 %collective-permute-start.18 = (f32[3,64,128]{2,1,0:T(8,128)S(1)}, f32[3,64,128]{2,1,0:T(8,128)S(1)}, u32[]{:S(2)}, u32[]{:S(2)}) collective-permute-start(f32[3,64,128]{2,1,0:T(8,128)S(1)} %add_add_fusion.6), channel_id=1, source_target_pairs={{0,8},{1,9},{2,10},{3,11},{4,12},{5,13},{6,14},{7,15},{8,0},{9,1},... | collective-permute-start | bytes 294920 | tf_op jit(solution)/shard_map/ppermute | solution.py:378
  57.6 9.7 %collective-permute-start.19 = (f32[3,64,128]{2,1,0:T(8,128)S(1)}, f32[3,64,128]{2,1,0:T(8,128)S(1)}, u32[]{:S(2)}, u32[]{:S(2)}) collective-permute-start(f32[3,64,128]{2,1,0:T(8,128)S(1)} %add_add_fusion.6), channel_id=1, source_target_pairs={{0,136},{1,137},{2,138},{3,139},{4,140},{5,141},{6,142},{7,143},{8... | collective-permute-start | bytes 294920 | tf_op jit(solution)/shard_map/ppermute | solution.py:378
  62.1 10.9 %collective-permute-start.8 = (f32[2,3,128,128]{3,2,1,0:T(8,128)S(1)}, f32[2,3,128,128]{3,2,1,0:T(8,128)S(1)}, u32[]{:S(2)}, u32[]{:S(2)}) collective-permute-start(f32[2,3,128,128]{3,2,1,0:T(8,128)S(1)} %get-tuple-element.59), channel_id=1, source_target_pairs={{0,32},{1,33},{2,34},{3,35},{4,36},{5,37},{6,38},{7,39},{8,40},{9,... | collective-permute-start | bytes 1179656 | tf_op jit(solution)/shard_map/ppermute | solution.py:370
  62.1 10.9 %collective-permute-start.9 = (f32[2,3,128,128]{3,2,1,0:T(8,128)S(1)}, f32[2,3,128,128]{3,2,1,0:T(8,128)S(1)}, u32[]{:S(2)}, u32[]{:S(2)}) collective-permute-start(f32[2,3,128,128]{3,2,1,0:T(8,128)S(1)} %get-tuple-element.60), channel_id=1, source_target_pairs={{0,224},{1,225},{2,226},{3,227},{4,228},{5,229},{6,230},{7,231},{8... | collective-permute-start | bytes 1179656 | tf_op jit(solution)/shard_map/ppermute | solution.py:370
  83.2 6.8 %collective-permute-start.28 = (f32[3,64,128]{2,1,0:T(8,128)S(1)}, f32[3,64,128]{2,1,0:T(8,128)S(1)}, u32[]{:S(2)}, u32[]{:S(2)}) collective-permute-start(f32[3,64,128]{2,1,0:T(8,128)S(1)} %add.128), channel_id=1, source_target_pairs={{0,64},{1,5},{2,66},{3,7},{4,68},{5,1},{6,70},{7,3},{8,72},{9,13},... | collective-permute-start | bytes 294920 | tf_op jit(solution)/shard_map/ppermute | solution.py:378
  85.9 8.8 %collective-permute-start.22 = (f32[2,192,128]{2,1,0:T(8,128)S(1)}, f32[2,192,128]{2,1,0:T(8,128)S(1)}, u32[]{:S(2)}, u32[]{:S(2)}) collective-permute-start(f32[2,192,128]{2,1,0:T(8,128)S(1)} %get-tuple-element.69), channel_id=1, source_target_pairs={{0,1},{1,2},{2,3},{3,4},{4,5},{5,6},{6,7},{7,8},{8,9},{9,10},{10,1... | collective-permute-start | bytes 589832 | tf_op jit(solution)/shard_map/ppermute | solution.py:370
  90.0 8.3 %collective-permute-start.23 = (f32[2,192,128]{2,1,0:T(8,128)S(1)}, f32[2,192,128]{2,1,0:T(8,128)S(1)}, u32[]{:S(2)}, u32[]{:S(2)}) collective-permute-start(f32[2,192,128]{2,1,0:T(8,128)S(1)} %get-tuple-element.70), channel_id=1, source_target_pairs={{0,31},{1,0},{2,1},{3,2},{4,3},{5,4},{6,5},{7,6},{8,7},{9,8},{10,9... | collective-permute-start | bytes 589832 | tf_op jit(solution)/shard_map/ppermute | solution.py:370
  90.0 8.9 %collective-permute-start.31 = (f32[3,64,128]{2,1,0:T(8,128)S(1)}, f32[3,64,128]{2,1,0:T(8,128)S(1)}, u32[]{:S(2)}, u32[]{:S(2)}) collective-permute-start(f32[3,64,128]{2,1,0:T(8,128)S(1)} %add_add_fusion.3), channel_id=1, source_target_pairs={{0,4},{1,65},{2,6},{3,67},{4,0},{5,69},{6,2},{7,71},{8,12},{9,73},... | collective-permute-start | bytes 294920 | tf_op jit(solution)/shard_map/ppermute | solution.py:378
  91.1 7.8 %collective-permute-start.32 = (f32[3,64,128]{2,1,0:T(8,128)S(1)}, f32[3,64,128]{2,1,0:T(8,128)S(1)}, u32[]{:S(2)}, u32[]{:S(2)}) collective-permute-start(f32[3,64,128]{2,1,0:T(8,128)S(1)} %add_add_fusion.3), channel_id=1, source_target_pairs={{0,6},{1,97},{2,4},{3,99},{4,2},{5,101},{6,0},{7,103},{8,14},{9,10... | collective-permute-start | bytes 294920 | tf_op jit(solution)/shard_map/ppermute | solution.py:378
  99.0 11.1 %collective-permute-start.34 = (f32[3,64,128]{2,1,0:T(8,128)S(1)}, f32[3,64,128]{2,1,0:T(8,128)S(1)}, u32[]{:S(2)}, u32[]{:S(2)}) collective-permute-start(f32[3,64,128]{2,1,0:T(8,128)S(1)} %add_add_fusion.2), channel_id=1, source_target_pairs={{0,8},{1,9},{2,10},{3,11},{4,12},{5,13},{6,14},{7,15},{8,0},{9,1},... | collective-permute-start | bytes 294920 | tf_op jit(solution)/shard_map/ppermute | solution.py:378
  102.6 7.5 %collective-permute-start.35 = (f32[3,64,128]{2,1,0:T(8,128)S(1)}, f32[3,64,128]{2,1,0:T(8,128)S(1)}, u32[]{:S(2)}, u32[]{:S(2)}) collective-permute-start(f32[3,64,128]{2,1,0:T(8,128)S(1)} %add_add_fusion.2), channel_id=1, source_target_pairs={{0,136},{1,137},{2,138},{3,139},{4,140},{5,141},{6,142},{7,143},{8... | collective-permute-start | bytes 294920 | tf_op jit(solution)/shard_map/ppermute | solution.py:378
  102.7 8.1 %collective-permute-start.33 = (f32[3,64,128]{2,1,0:T(8,128)S(1)}, f32[3,64,128]{2,1,0:T(8,128)S(1)}, u32[]{:S(2)}, u32[]{:S(2)}) collective-permute-start(f32[3,64,128]{2,1,0:T(8,128)S(1)} %add_add_fusion.2), channel_id=1, source_target_pairs={{0,128},{1,129},{2,130},{3,131},{4,132},{5,133},{6,134},{7,135},{8... | collective-permute-start | bytes 294920 | tf_op jit(solution)/shard_map/ppermute | solution.py:378
  103.0 14.3 %collective-permute-start.24 = (f32[2,3,64,128]{3,2,1,0:T(8,128)S(1)}, f32[2,3,64,128]{3,2,1,0:T(8,128)S(1)}, u32[]{:S(2)}, u32[]{:S(2)}) collective-permute-start(f32[2,3,64,128]{3,2,1,0:T(8,128)S(1)} %get-tuple-element.72), channel_id=1, source_target_pairs={{0,32},{1,33},{2,34},{3,35},{4,36},{5,37},{6,38},{7,39},{8,40},{9,... | collective-permute-start | bytes 589832 | tf_op jit(solution)/shard_map/ppermute | solution.py:370
  103.9 13.3 %collective-permute-start.25 = (f32[2,3,64,128]{3,2,1,0:T(8,128)S(1)}, f32[2,3,64,128]{3,2,1,0:T(8,128)S(1)}, u32[]{:S(2)}, u32[]{:S(2)}) collective-permute-start(f32[2,3,64,128]{3,2,1,0:T(8,128)S(1)} %get-tuple-element.73), channel_id=1, source_target_pairs={{0,224},{1,225},{2,226},{3,227},{4,228},{5,229},{6,230},{7,231},{8... | collective-permute-start | bytes 589832 | tf_op jit(solution)/shard_map/ppermute | solution.py:370
  110.8 8.3 %collective-permute-start.36 = (f32[3,64,128]{2,1,0:T(8,128)S(1)}, f32[3,64,128]{2,1,0:T(8,128)S(1)}, u32[]{:S(2)}, u32[]{:S(2)}) collective-permute-start(f32[3,64,128]{2,1,0:T(8,128)S(1)} %add_add_fusion.1), channel_id=1, source_target_pairs={{0,152},{1,153},{2,154},{3,155},{4,156},{5,157},{6,158},{7,159},{8... | collective-permute-start | bytes 294920 | tf_op jit(solution)/shard_map/ppermute | solution.py:378
  (20 other events, 112.3 us)
